TPU v7x, 32 devices: a whole 2x2x4 slice. The times are simulated.
32 devices in a mesh: dp: 8 (over y, x, core), tensor: 4 (over z).
Axes of the slice: x: 2, y: 2, z: 4, core: 2. Of those that a mesh axis runs over, the one named last changes fastest.
Arguments:
- tokens: bfloat16 [4096, 896], P(('dp', 'tensor')), parts along dimension 0, may hold values from -6 to 6
- smooth_scale: float32 [896], replicated, may hold values from 0.25 to 4
- gate_weight: bfloat16 [4864, 896], P('tensor'), may hold values from -0.1875 to 0.1875
- up_weight: bfloat16 [4864, 896], P('tensor'), may hold values from -0.1875 to 0.1875
- down_weight: bfloat16 [4864, 896], P('tensor'), may hold values from -0.078125 to 0.078125
Outputs:
- mixed: bfloat16 [4096, 896], P(('dp', 'tensor')), parts along dimension 0
There are 8 independent parts, one for each index of `dp`. A program takes and returns all parts, laid end to end along the dimension named above; an argument that names none is the same for every part. Nothing has to cross between parts.
All inputs are finite; a program needn't handle non-finite values.
Results may differ from a plain program's by a relative error of at most 0.0064.
Values may be sent and summed in bfloat16 or wider, within the bound.
No kernel may reach another device: no remote copies, remote signals or barrier semaphores. Data moves between devices by JAX's collectives and lax.ppermute only.
A program may use at most 64 MiB of HBM per device.

v0:
```python
import jax
import jax.numpy as jnp
from jax import lax
from jax.sharding import PartitionSpec as P


def from_behind(block, axis, distance):
    devices = range(lax.axis_size(axis))
    route = [((i - distance) % len(devices), i) for i in devices]
    return lax.ppermute(block, axis, route)


def shards(tokens, smooth_scale, gate_weight, up_weight, down_weight):
    smoothed = (tokens.astype(jnp.float32) / smooth_scale[None, :]).astype(jnp.bfloat16)
    row_count = tokens.shape[0]
    contract = (((1,), (1,)), ((), ()))
    row_piece = lax.all_gather(smoothed, "tensor", axis=0, tiled=True)
    gate_out = lax.dot_general(row_piece, gate_weight, contract, preferred_element_type=jnp.float32)
    up_out = lax.dot_general(row_piece, up_weight, contract, preferred_element_type=jnp.float32)
    hidden = (jax.nn.silu(gate_out) * up_out).astype(jnp.bfloat16)
    devices_n = lax.axis_size("tensor")
    position = lax.axis_index("tensor")

    def partial_for(block_index):
        block_start = (block_index + 2 * devices_n) % devices_n * row_count
        block_rows = lax.dynamic_slice_in_dim(hidden, block_start, row_count, 0)
        return jnp.dot(block_rows, down_weight, preferred_element_type=jnp.float32)

    def forward_hop(hop_index, carried):
        moved = from_behind(carried, "tensor", 1)
        return moved + partial_for(position - 1 - hop_index)

    summed = lax.fori_loop(1, devices_n, forward_hop, partial_for(position - 1))
    return summed.astype(jnp.bfloat16)


def solution(mesh):
    return jax.shard_map(
        shards,
        mesh=mesh,
        in_specs=(
            P(("dp", "tensor"), None),
            P(),
            P("tensor", None),
            P("tensor", None),
            P("tensor", None),
        ),
        out_specs=P(("dp", "tensor"), None),
        check_vma=False,
    )
```

profile of v0, /device:TPU:0, one launch (start us, length us, event | category | flops | bytes accessed | tf_op | source)
XLA Modules:
  0.0 70.6 jit_solution(15943051984502532566)
XLA Ops:
  0.0 0.0 copy-start
  0.0 1.1 %divide_convert_fusion = bf16[128,896]{1,0:T(8,128)(2,1)S(1)} fusion(bf16[128,896]{1,0:T(8,128)(2,1)} %param.7, f32[896]{0:T(1024)} %param.8), kind=kLoop, calls=%fused_computation.5 | loop fusion | flops 344064 | bytes 462336 | tf_op jit(solution)/shard_map/convert_element_type | solution.py:14
  1.1 22.8 %all_gather.3 = bf16[512,896]{1,0:T(8,128)(2,1)S(1)} all-gather(bf16[128,896]{1,0:T(8,128)(2,1)S(1)} %divide_convert_fusion), channel_id=1, replica_groups=mesh['dp'=8,'tensor'=4] {'tensor'}, dimensions={0}, use_global_device_ids=true | all-gather | bytes 1146880 | tf_op jit(solution)/shard_map/all_gather | solution.py:17
  23.9 0.0 copy-done
  23.9 0.0 copy-start.1
  23.9 1.5 %fusion.6 = f32[512,1216]{0,1:T(8,128)S(1)} fusion(bf16[512,896]{1,0:T(8,128)(2,1)S(1)} %all_gather.3, bf16[1216,896]{1,0:T(8,128)(2,1)S(1)} %copy-done), kind=kOutput, calls=%fused_computation.9 | convolution fusion | flops 1115684864 | bytes 5586944 | tf_op jit(solution)/shard_map/dot_general | solution.py:18
  25.4 0.1 copy-done.1
  25.5 2.9 %fusion.2 = bf16[512,1216]{0,1:T(8,128)(2,1)} fusion(bf16[512,896]{1,0:T(8,128)(2,1)S(1)} %all_gather.3, bf16[1216,896]{1,0:T(8,128)(2,1)S(1)} %copy-done.1, f32[512,1216]{0,1:T(8,128)S(1)} %fusion.6), kind=kOutput, calls=%fused_computation.4 | convolution fusion | flops 1119420416 | bytes 6832128 | tf_op jit(solution)/shard_map/dot_general | solution.py:19
  28.4 2.3 %fusion.3 = f32[128,896]{1,0:T(8,128)S(1)} fusion(bf16[1216,896]{1,0:T(8,128)(2,1)} %param.11, bf16[512,1216]{0,1:T(8,128)(2,1)} %fusion.2, s32[]{:T(128)S(6)} %select_n.38), kind=kOutput, calls=%fused_computation.6 | convolution fusion | flops 278921216 | bytes 2949124 | tf_op jit(solution)/shard_map/dot_general | solution.py:27
  30.6 39.2 %while.15 = (s32[]{:T(128)}, f32[128,896]{1,0:T(8,128)S(1)}, s32[]{:T(128)}, bf16[512,1216]{0,1:T(8,128)(2,1)}, bf16[1216,896]{1,0:T(8,128)(2,1)}, /*index=5*/s3...) while((s32[]{:T(128)}, f32[128,896]{1,0:T(8,128)S(1)}, ...), condition=%wide.region_1.2_spmd, body=%wide.region_0.1_spmd.sunk | while | flops 279035936 | bytes 5243220 | solution.py:33
  30.7 0.1 collective-permute-start
  30.8 11.4 %collective-permute-done = f32[128,896]{1,0:T(8,128)S(1)} collective-permute-done((f32[128,896]{1,0:T(8,128)S(1)}, f32[128,896]{1,0:T(8,128)S(1)}, u32[]{:S(2)}, u32[]{:S(2)}) %collective-permute-start) | collective-permute-done | bytes 458784 | tf_op jit(solution)/shard_map/while/body/eval_jaxpr/ppermute | solution.py:10
  42.1 2.3 %convolution_add_fusion.2 = f32[128,896]{1,0:T(8,128)S(1)} fusion(f32[128,896]{1,0:T(8,128)S(1)} %collective-permute-done, bf16[1216,896]{1,0:T(8,128)(2,1)} %get-tuple-element.216, bf16[512,1216]{0,1:T(8,128)(2,1)} %get-tuple-element.215, s32[]{:T(128)S(6)} %select_n.42), kind=kOutput, calls=%fused_computation.clone.1 | convolution fusion | flops 279035904 | bytes 3407876 | tf_op jit(solution)/shard_map/while/body/eval_jaxpr/dot_general | solution.py:27
  44.4 0.1 collective-permute-start
  44.5 10.4 %collective-permute-done = f32[128,896]{1,0:T(8,128)S(1)} collective-permute-done((f32[128,896]{1,0:T(8,128)S(1)}, f32[128,896]{1,0:T(8,128)S(1)}, u32[]{:S(2)}, u32[]{:S(2)}) %collective-permute-start) | collective-permute-done | bytes 458784 | tf_op jit(solution)/shard_map/while/body/eval_jaxpr/ppermute | solution.py:10
  54.9 2.3 %convolution_add_fusion.2 = f32[128,896]{1,0:T(8,128)S(1)} fusion(f32[128,896]{1,0:T(8,128)S(1)} %collective-permute-done, bf16[1216,896]{1,0:T(8,128)(2,1)} %get-tuple-element.216, bf16[512,1216]{0,1:T(8,128)(2,1)} %get-tuple-element.215, s32[]{:T(128)S(6)} %select_n.42), kind=kOutput, calls=%fused_computation.clone.1 | convolution fusion | flops 279035904 | bytes 3407876 | tf_op jit(solution)/shard_map/while/body/eval_jaxpr/dot_general | solution.py:27
  57.2 0.1 collective-permute-start
  57.3 10.2 %collective-permute-done = f32[128,896]{1,0:T(8,128)S(1)} collective-permute-done((f32[128,896]{1,0:T(8,128)S(1)}, f32[128,896]{1,0:T(8,128)S(1)}, u32[]{:S(2)}, u32[]{:S(2)}) %collective-permute-start) | collective-permute-done | bytes 458784 | tf_op jit(solution)/shard_map/while/body/eval_jaxpr/ppermute | solution.py:10
  67.6 2.3 %convolution_add_fusion.2 = f32[128,896]{1,0:T(8,128)S(1)} fusion(f32[128,896]{1,0:T(8,128)S(1)} %collective-permute-done, bf16[1216,896]{1,0:T(8,128)(2,1)} %get-tuple-element.216, bf16[512,1216]{0,1:T(8,128)(2,1)} %get-tuple-element.215, s32[]{:T(128)S(6)} %select_n.42), kind=kOutput, calls=%fused_computation.clone.1 | convolution fusion | flops 279035904 | bytes 3407876 | tf_op jit(solution)/shard_map/while/body/eval_jaxpr/dot_general | solution.py:27
  69.9 0.7 %convert_element_type.15 = bf16[128,896]{1,0:T(8,128)(2,1)} convert(f32[128,896]{1,0:T(8,128)S(1)} %get-tuple-element.141) | non-fusion elementwise | flops 114688 | bytes 688128 | tf_op jit(solution)/shard_map/convert_element_type | solution.py:34
Async XLA Ops:
  0.0 23.9 %copy-start = (bf16[1216,896]{1,0:T(8,128)(2,1)S(1)}, bf16[1216,896]{1,0:T(8,128)(2,1)}, u32[]{:S(2)}) copy-start(bf16[1216,896]{1,0:T(8,128)(2,1)} %param.9) | copy-start | bytes 6537220
  23.9 1.6 %copy-start.1 = (bf16[1216,896]{1,0:T(8,128)(2,1)S(1)}, bf16[1216,896]{1,0:T(8,128)(2,1)}, u32[]{:S(2)}) copy-start(bf16[1216,896]{1,0:T(8,128)(2,1)} %param.10) | copy-start | bytes 6537220
  30.7 11.5 %collective-permute-start = (f32[128,896]{1,0:T(8,128)S(1)}, f32[128,896]{1,0:T(8,128)S(1)}, u32[]{:S(2)}, u32[]{:S(2)}) collective-permute-start(f32[128,896]{1,0:T(8,128)S(1)} %get-tuple-element.201), channel_id=1, source_target_pairs={{3,0},{0,1},{1,2},{2,3},{7,4},{4,5},{5,6},{6,7},{11,8},{8,9},{9,10... | collective-permute-start | bytes 1376264 | tf_op jit(solution)/shard_map/while/body/eval_jaxpr/ppermute | solution.py:10
  44.4 10.5 %collective-permute-start = (f32[128,896]{1,0:T(8,128)S(1)}, f32[128,896]{1,0:T(8,128)S(1)}, u32[]{:S(2)}, u32[]{:S(2)}) collective-permute-start(f32[128,896]{1,0:T(8,128)S(1)} %get-tuple-element.201), channel_id=1, source_target_pairs={{3,0},{0,1},{1,2},{2,3},{7,4},{4,5},{5,6},{6,7},{11,8},{8,9},{9,10... | collective-permute-start | bytes 1376264 | tf_op jit(solution)/shard_map/while/body/eval_jaxpr/ppermute | solution.py:10
  57.2 10.3 %collective-permute-start = (f32[128,896]{1,0:T(8,128)S(1)}, f32[128,896]{1,0:T(8,128)S(1)}, u32[]{:S(2)}, u32[]{:S(2)}) collective-permute-start(f32[128,896]{1,0:T(8,128)S(1)} %get-tuple-element.201), channel_id=1, source_target_pairs={{3,0},{0,1},{1,2},{2,3},{7,4},{4,5},{5,6},{6,7},{11,8},{8,9},{9,10... | collective-permute-start | bytes 1376264 | tf_op jit(solution)/shard_map/while/body/eval_jaxpr/ppermute | solution.py:10
where the time goes:
time: 70.9 us; the launch traced here: 70.6 us
  waiting for transfers between devices  32 us (45%)
  blocking collectives  22.8 us (32%)
  matrix products  13.5 us (19%)
  other arithmetic  1.85 us (3%)
    ppermute x3, waiting for transfers between devices, from_behind(): return lax.ppermute(block, axis, route)  32 us
    all_gather x1, blocking collectives, shards(): row_piece = lax.all_gather(smoothed, 'tensor', axis=0, tiled=True)  22.8 us
    dot_general x4, matrix products, partial_for(): return jnp.dot(block_rows, down_weight, preferred_element_type=jnp.float32)  9.1 us
    dot_general x1, matrix products, shards(): lax.dot_general(row_piece, up_weight, contract, preferred_element_type=jn...  2.85 us
    dot_general x1, matrix products, shards(): lax.dot_general(row_piece, gate_weight, contract, preferred_element_type=...  1.51 us
  transfers between devices with their start and end apart: 3, of which 3 were waited for; matrix products, arithmetic and copies ran while one was open for 0% of the time, Pallas kernels for 0%

commit v1 on v0

v1 whole, which is shorter than its diff:
```python
import functools

import jax
import jax.numpy as jnp
from jax import lax
from jax.experimental import pallas as pl
from jax.experimental.pallas import tpu as pltpu
from jax.sharding import PartitionSpec as P

UNIT_TILE = 256
CONTRACT_LAST = (((1,), (1,)), ((), ()))
VMEM_LIMIT = 16 * 2**20
OWN_VMEM_LIMIT = 46 * 2**20
VMEM_SPEC = pl.BlockSpec(memory_space=pltpu.VMEM)
HBM_SPEC = pl.BlockSpec(memory_space=pltpu.HBM)


def unit_tiles(units):
    return [pl.ds(start, min(UNIT_TILE, units - start)) for start in range(0, units, UNIT_TILE)]


def hidden_tile(x, gate, up):
    gate_out = lax.dot_general(x, gate, CONTRACT_LAST, preferred_element_type=jnp.float32)
    up_out = lax.dot_general(x, up, CONTRACT_LAST, preferred_element_type=jnp.float32)
    return (gate_out / (1.0 + jnp.exp(-gate_out)) * up_out).astype(jnp.bfloat16)


def smooth(x, scale):
    return (x.astype(jnp.float32) / scale).astype(jnp.bfloat16)


def own_kernel(x_ref, scale_ref, gate_hbm, up_hbm, down_hbm, out_ref, gate_ref, up_ref, down_ref, hidden, sems):
    tiles = unit_tiles(gate_hbm.shape[0])
    copies = [
        [
            pltpu.make_async_copy(source.at[tile, :], target.at[tile, :], sems.at[which, index])
            for which, (source, target) in enumerate(((gate_hbm, gate_ref), (up_hbm, up_ref)))
        ]
        for index, tile in enumerate(tiles)
    ]
    down_copy = pltpu.make_async_copy(down_hbm, down_ref, sems.at[2, 0])
    for pair in copies:
        for copy in pair:
            copy.start()
    down_copy.start()
    x = smooth(x_ref[...], scale_ref[...])
    for pair, tile in zip(copies, tiles):
        for copy in pair:
            copy.wait()
        hidden[:, tile] = hidden_tile(x, gate_ref[tile, :], up_ref[tile, :])
    down_copy.wait()
    out_ref[...] = jnp.dot(hidden[...], down_ref[...], preferred_element_type=jnp.float32)


def arrived_kernel(x_ref, scale_ref, gate_ref, up_ref, down_ref, out_ref, hidden):
    x = smooth(x_ref[...], scale_ref[...])
    for tile in unit_tiles(gate_ref.shape[0]):
        hidden[:, tile] = hidden_tile(x, gate_ref[tile, :], up_ref[tile, :])
    out_ref[...] = jnp.dot(hidden[...], down_ref[...], preferred_element_type=jnp.float32).astype(out_ref.dtype)


def cost(rows, width, units):
    return pl.CostEstimate(flops=6 * rows * width * units, bytes_accessed=6 * units * width, transcendentals=2 * rows * units)


def own_block(x, scale, weights):
    rows, width = x.shape
    units = weights[0].shape[0]
    held = tuple(jax.ShapeDtypeStruct(w.shape, w.dtype) for w in weights)
    part, *kept = pl.pallas_call(
        own_kernel,
        out_shape=(jax.ShapeDtypeStruct((rows, width), jnp.float32),) + held,
        in_specs=[VMEM_SPEC] * 2 + [HBM_SPEC] * 3,
        out_specs=(VMEM_SPEC,) * 4,
        scratch_shapes=[pltpu.VMEM((rows, units), jnp.bfloat16), pltpu.SemaphoreType.DMA((3, len(unit_tiles(units))))],
        compiler_params=pltpu.CompilerParams(vmem_limit_bytes=OWN_VMEM_LIMIT),
        cost_estimate=cost(rows, width, units),
        name="own_block",
    )(x, scale, *weights)
    return part, kept


def arrived_block(x, scale, weights, dtype):
    rows, width = x.shape
    units = weights[0].shape[0]
    return pl.pallas_call(
        arrived_kernel,
        out_shape=jax.ShapeDtypeStruct((rows, width), dtype),
        in_specs=[VMEM_SPEC] * 5,
        out_specs=VMEM_SPEC,
        scratch_shapes=[pltpu.VMEM((rows, units), jnp.bfloat16)],
        compiler_params=pltpu.CompilerParams(vmem_limit_bytes=VMEM_LIMIT),
        cost_estimate=cost(rows, width, units),
        name="arrived_block",
    )(x, scale, *weights)


def shards(tokens, smooth_scale, gate_weight, up_weight, down_weight):
    n = lax.axis_size("tensor")
    ring = list(range(0, n, 2)) + list(range(1, n, 2))[::-1]
    route = [(ring[k - 1], ring[k]) for k in range(n)]
    send = functools.partial(lax.ppermute, axis_name="tensor", perm=route)
    scale = smooth_scale[None, :]
    own, weights = own_block(tokens, scale, (gate_weight, up_weight, down_weight))
    x, summed = tokens, None
    for hop in range(1, n):
        x = send(x)
        if hop == 1:
            summed = arrived_block(x, scale, weights, jnp.bfloat16)
        else:
            part = arrived_block(x, scale, weights, jnp.float32)
            summed = (send(summed).astype(jnp.float32) + part).astype(jnp.bfloat16)
    if n > 1:
        own = own + send(summed).astype(jnp.float32)
    return own.astype(jnp.bfloat16)


def solution(mesh):
    return jax.shard_map(
        shards,
        mesh=mesh,
        in_specs=(
            P(("dp", "tensor"), None),
            P(),
            P("tensor", None),
            P("tensor", None),
            P("tensor", None),
        ),
        out_specs=P(("dp", "tensor"), None),
        check_vma=False,
    )
```

time: 70.9 us -> 39.2 us (0.55)
  blocking collectives: 22.8 us -> 0 us
  waiting for transfers between devices: 32 us -> 9.69 us
  starting transfers between devices: 0.18 us -> 17.1 us
  matrix products: 13.5 us -> 0 us
  Pallas kernels: 0 us -> 9.73 us
  local copies, waits for them, and re-layouts: 0.11 us -> 1.63 us
  other arithmetic: 1.85 us -> 0.81 us
    all_gather x1 -> x0, blocking collectives: 22.8 us -> none  [shards(): row_piece = lax.all_gather(smoothed, 'tensor', axis=0, tiled=True)]
    ppermute x3 -> x6, waiting for transfers between devices: 32 us -> 9.69 us  [the longest x3 4.85 us: shards(): x = send(x)]
    ppermute x3 -> x6, starting transfers between devices: 0.18 us -> 17.1 us  [the longest x3 10.2 us: shards(): x = send(x)]
    dot_general x6 -> x0, matrix products: 13.5 us -> none  [the longest x4 9.1 us: partial_for(): return jnp.dot(block_rows, down_weight, preferred_element_type=jnp.float32)]
    pallas_call x0 -> x4, Pallas kernels: none -> 9.73 us  [the longest x3 5.7 us: arrived_block(): pl.pallas_call(arrived_kernel, out_shape=jax.ShapeDtypeStruct((rows, widt...]
    convert_element_type x2 -> x3, other arithmetic: 1.85 us -> 0.81 us  [the longest x1 0.73 us: shards(): return own.astype(jnp.bfloat16)]
    unnamed x4 -> x2, local copies, waits for them, and re-layouts: 0.11 us -> 0.94 us
  transfers between devices with their start and end apart: 3 -> 6, of which waited for: 3 -> 4; matrix products, arithmetic and copies ran while one was open for 0% -> 2% of each run, Pallas kernels for 0% -> 25%
where the time goes in v1:
time: 39.2 us; the launch traced here: 39 us
  starting transfers between devices  17.1 us (44%)
  Pallas kernels  9.73 us (25%)
  waiting for transfers between devices  9.69 us (25%)
  local copies, waits for them, and re-layouts  1.63 us (4%)
  other arithmetic  0.81 us (2%)
    ppermute x3, starting transfers between devices, shards(): x = send(x)  10.2 us
    pallas_call x3, Pallas kernels, arrived_block(): pl.pallas_call(arrived_kernel, out_shape=jax.ShapeDtypeStruct((rows, widt...  5.7 us
    ppermute x3, waiting for transfers between devices, shards(): x = send(x)  4.85 us
    pallas_call x1, Pallas kernels, own_block(): pl.pallas_call(own_kernel, out_shape=(jax.ShapeDtypeStruct((rows, width),...  4.03 us
    ppermute x2, starting transfers between devices, shards(): summed = (send(summed).astype(jnp.float32) + part).astype(jnp.bfloat16)  3.79 us
    ppermute x1, waiting for transfers between devices, shards(): own = own + send(summed).astype(jnp.float32)  3.54 us
    ppermute x1, starting transfers between devices, shards(): own = own + send(summed).astype(jnp.float32)  3.08 us
    ppermute x2, waiting for transfers between devices, shards(): summed = (send(summed).astype(jnp.float32) + part).astype(jnp.bfloat16)  1.29 us
  transfers between devices with their start and end apart: 6, of which 4 were waited for; matrix products, arithmetic and copies ran while one was open for 2% of the time, Pallas kernels for 25%

profile of v1, /device:TPU:0, one launch (start us, length us, event | category | flops | bytes accessed | tf_op | source)
XLA Modules:
  0.0 39.0 jit_solution(3626612192525327899)
XLA Ops:
  0.0 4.0 %collective-permute-start = (bf16[128,896]{1,0:T(8,128)(2,1)}, bf16[128,896]{1,0:T(8,128)(2,1)S(1)}, u32[]{:S(2)}, u32[]{:S(2)}) collective-permute-start(bf16[128,896]{1,0:T(8,128)(2,1)} %x_ref.1), channel_id=1, source_target_pairs={{1,0},{0,2},{2,3},{3,1},{5,4},{4,6},{6,7},{7,5},{9,8},{8,10},{10,1... | collective-permute-start | bytes 688136 | tf_op jit(solution)/shard_map/ppermute | solution.py:107
  4.0 0.7 %broadcast_in_dim.3.scale_ref = f32[1,896]{1,0:T(1,128)S(1)} reshape(f32[896]{0:T(1024)} %param.6) | data formatting | bytes 7168 | tf_op jit(solution)/shard_map/broadcast_in_dim | solution.py:103
  4.7 0.0 copy-start
  4.7 0.9 %copy-done = bf16[128,896]{1,0:T(8,128)(2,1)S(1)} copy-done((bf16[128,896]{1,0:T(8,128)(2,1)S(1)}, bf16[128,896]{1,0:T(8,128)(2,1)}, u32[]{:S(2)}) %copy-start) | copy-done | bytes 229400
  5.7 4.0 %own_block.1 = (f32[128,896]{1,0:T(8,128)S(1)}, bf16[1216,896]{1,0:T(8,128)(2,1)S(1)}, bf16[1216,896]{1,0:T(8,128)(2,1)S(1)}, bf16[1216,896]{1,0:T(8,128)(2,1)S(1)}) custom-call(bf16[128,896]{1,0:T(8,128)(2,1)S(1)} %copy-done, f32[1,896]{1,0:T(1,128)S(1)} %broadcast_in_dim.3.scale_ref, bf16[1216,896]{1,0:T(8,128)(2,1)} %gate_hbm.1, ...), custom_call_target="tpu_custom_call" | custom-call | flops 836763648 | bytes 6537216 | tf_op jit(solution)/shard_map/own_block/pallas_call | solution.py:70
  9.7 0.0 collective-permute-done.x_ref
  9.7 2.8 %collective-permute-start.2 = (bf16[128,896]{1,0:T(8,128)(2,1)S(1)}, bf16[128,896]{1,0:T(8,128)(2,1)S(1)}, u32[]{:S(2)}, u32[]{:S(2)}) collective-permute-start(bf16[128,896]{1,0:T(8,128)(2,1)S(1)} %collective-permute-done.x_ref), channel_id=1, source_target_pairs={{1,0},{0,2},{2,3},{3,1},{5,4},{4,6},{6,7},{7,5},{9,8},{8,10},{10,1... | collective-permute-start | bytes 688136 | tf_op jit(solution)/shard_map/ppermute | solution.py:107
  12.5 1.9 %arrived_block.3 = bf16[128,896]{1,0:T(8,128)(2,1)S(1)} custom-call(bf16[128,896]{1,0:T(8,128)(2,1)S(1)} %collective-permute-done.x_ref, f32[1,896]{1,0:T(1,128)S(1)} %broadcast_in_dim.3.scale_ref, bf16[1216,896]{1,0:T(8,128)(2,1)S(1)} %get-tuple-element.10.gate_ref, bf16[1216,896]{1,0:T(8,128)(2,1)S(1)} %get-tuple-element.11.up_ref, ...), custom_call_target="tpu_custom_call" | custom-call | flops 836763648 | bytes 6537216 | tf_op jit(solution)/shard_map/arrived_block/pallas_call | solution.py:86
  14.4 0.7 %collective-permute-start.1 = (bf16[128,896]{1,0:T(8,128)(2,1)S(1)}, bf16[128,896]{1,0:T(8,128)(2,1)S(1)}, u32[]{:S(2)}, u32[]{:S(2)}) collective-permute-start(bf16[128,896]{1,0:T(8,128)(2,1)S(1)} %arrived_block.3), channel_id=1, source_target_pairs={{1,0},{0,2},{2,3},{3,1},{5,4},{4,6},{6,7},{7,5},{9,8},{8,10},{10,1... | collective-permute-start | bytes 688136 | tf_op jit(solution)/shard_map/ppermute | solution.py:112
  15.1 3.4 %collective-permute-done.2.x_ref = bf16[128,896]{1,0:T(8,128)(2,1)S(1)} collective-permute-done((bf16[128,896]{1,0:T(8,128)(2,1)S(1)}, bf16[128,896]{1,0:T(8,128)(2,1)S(1)}, u32[]{:S(2)}, u32[]{:S(2)}) %collective-permute-start.2) | collective-permute-done | bytes 229408 | tf_op jit(solution)/shard_map/ppermute | solution.py:107
  18.6 3.4 %collective-permute-start.4 = (bf16[128,896]{1,0:T(8,128)(2,1)S(1)}, bf16[128,896]{1,0:T(8,128)(2,1)S(1)}, u32[]{:S(2)}, u32[]{:S(2)}) collective-permute-start(bf16[128,896]{1,0:T(8,128)(2,1)S(1)} %collective-permute-done.2.x_ref), channel_id=1, source_target_pairs={{1,0},{0,2},{2,3},{3,1},{5,4},{4,6},{6,7},{7,5},{9,8},{8,10},{10,1... | collective-permute-start | bytes 688136 | tf_op jit(solution)/shard_map/ppermute | solution.py:107
  21.9 1.9 %arrived_block.4 = f32[128,896]{1,0:T(8,128)S(1)} custom-call(bf16[128,896]{1,0:T(8,128)(2,1)S(1)} %collective-permute-done.2.x_ref, f32[1,896]{1,0:T(1,128)S(1)} %broadcast_in_dim.3.scale_ref, bf16[1216,896]{1,0:T(8,128)(2,1)S(1)} %get-tuple-element.10.gate_ref, bf16[1216,896]{1,0:T(8,128)(2,1)S(1)} %get-tuple-element.11.up_ref, ...), custom_call_target="tpu_custom_call" | custom-call | flops 836763648 | bytes 6537216 | tf_op jit(solution)/shard_map/arrived_block/pallas_call | solution.py:86
  23.8 0.0 collective-permute-done.1
  23.9 3.0 %collective-permute-start.3 = (bf16[128,896]{1,0:T(8,128)(2,1)S(1)}, bf16[128,896]{1,0:T(8,128)(2,1)S(1)}, u32[]{:S(2)}, u32[]{:S(2)}) collective-permute-start(bf16[128,896]{1,0:T(8,128)(2,1)S(1)} %add_convert_fusion.2), channel_id=1, source_target_pairs={{1,0},{0,2},{2,3},{3,1},{5,4},{4,6},{6,7},{7,5},{9,8},{8,10},{10,1... | collective-permute-start | bytes 688136 | tf_op jit(solution)/shard_map/ppermute | solution.py:112
  26.9 1.4 %collective-permute-done.4.x_ref = bf16[128,896]{1,0:T(8,128)(2,1)S(1)} collective-permute-done((bf16[128,896]{1,0:T(8,128)(2,1)S(1)}, bf16[128,896]{1,0:T(8,128)(2,1)S(1)}, u32[]{:S(2)}, u32[]{:S(2)}) %collective-permute-start.4) | collective-permute-done | bytes 229408 | tf_op jit(solution)/shard_map/ppermute | solution.py:107
  28.4 1.9 %arrived_block.5 = f32[128,896]{1,0:T(8,128)S(1)} custom-call(bf16[128,896]{1,0:T(8,128)(2,1)S(1)} %collective-permute-done.4.x_ref, f32[1,896]{1,0:T(1,128)S(1)} %broadcast_in_dim.3.scale_ref, bf16[1216,896]{1,0:T(8,128)(2,1)S(1)} %get-tuple-element.10.gate_ref, bf16[1216,896]{1,0:T(8,128)(2,1)S(1)} %get-tuple-element.11.up_ref, ...), custom_call_target="tpu_custom_call" | custom-call | flops 836763648 | bytes 6537216 | tf_op jit(solution)/shard_map/arrived_block/pallas_call | solution.py:86
  30.3 1.3 %collective-permute-done.3 = bf16[128,896]{1,0:T(8,128)(2,1)S(1)} collective-permute-done((bf16[128,896]{1,0:T(8,128)(2,1)S(1)}, bf16[128,896]{1,0:T(8,128)(2,1)S(1)}, u32[]{:S(2)}, u32[]{:S(2)}) %collective-permute-start.3) | collective-permute-done | bytes 229408 | tf_op jit(solution)/shard_map/ppermute | solution.py:112
  31.6 3.1 %collective-permute-start.5 = (bf16[128,896]{1,0:T(8,128)(2,1)S(1)}, bf16[128,896]{1,0:T(8,128)(2,1)S(1)}, u32[]{:S(2)}, u32[]{:S(2)}) collective-permute-start(bf16[128,896]{1,0:T(8,128)(2,1)S(1)} %add_convert_fusion.1), channel_id=1, source_target_pairs={{1,0},{0,2},{2,3},{3,1},{5,4},{4,6},{6,7},{7,5},{9,8},{8,10},{10,1... | collective-permute-start | bytes 688136 | tf_op jit(solution)/shard_map/ppermute | solution.py:114
  34.7 3.5 %collective-permute-done.5 = bf16[128,896]{1,0:T(8,128)(2,1)S(1)} collective-permute-done((bf16[128,896]{1,0:T(8,128)(2,1)S(1)}, bf16[128,896]{1,0:T(8,128)(2,1)S(1)}, u32[]{:S(2)}, u32[]{:S(2)}) %collective-permute-start.5) | collective-permute-done | bytes 229408 | tf_op jit(solution)/shard_map/ppermute | solution.py:114
  38.2 0.7 %add_convert_fusion = bf16[128,896]{1,0:T(8,128)(2,1)} fusion(f32[128,896]{1,0:T(8,128)S(1)} %get-tuple-element.9, bf16[128,896]{1,0:T(8,128)(2,1)S(1)} %collective-permute-done.5), kind=kLoop, calls=%fused_computation | loop fusion | flops 344064 | bytes 917504 | tf_op jit(solution)/shard_map/convert_element_type | solution.py:115
  (2 shorter events, 0.1 us)
Async XLA Ops:
  0.0 9.7 %collective-permute-start = (bf16[128,896]{1,0:T(8,128)(2,1)}, bf16[128,896]{1,0:T(8,128)(2,1)S(1)}, u32[]{:S(2)}, u32[]{:S(2)}) collective-permute-start(bf16[128,896]{1,0:T(8,128)(2,1)} %x_ref.1), channel_id=1, source_target_pairs={{1,0},{0,2},{2,3},{3,1},{5,4},{4,6},{6,7},{7,5},{9,8},{8,10},{10,1... | collective-permute-start | bytes 688136 | tf_op jit(solution)/shard_map/ppermute | solution.py:107
  4.7 0.9 %copy-start = (bf16[128,896]{1,0:T(8,128)(2,1)S(1)}, bf16[128,896]{1,0:T(8,128)(2,1)}, u32[]{:S(2)}) copy-start(bf16[128,896]{1,0:T(8,128)(2,1)} %x_ref.1) | copy-start | bytes 688132
  9.7 8.8 %collective-permute-start.2 = (bf16[128,896]{1,0:T(8,128)(2,1)S(1)}, bf16[128,896]{1,0:T(8,128)(2,1)S(1)}, u32[]{:S(2)}, u32[]{:S(2)}) collective-permute-start(bf16[128,896]{1,0:T(8,128)(2,1)S(1)} %collective-permute-done.x_ref), channel_id=1, source_target_pairs={{1,0},{0,2},{2,3},{3,1},{5,4},{4,6},{6,7},{7,5},{9,8},{8,10},{10,1... | collective-permute-start | bytes 688136 | tf_op jit(solution)/shard_map/ppermute | solution.py:107
  14.4 9.4 %collective-permute-start.1 = (bf16[128,896]{1,0:T(8,128)(2,1)S(1)}, bf16[128,896]{1,0:T(8,128)(2,1)S(1)}, u32[]{:S(2)}, u32[]{:S(2)}) collective-permute-start(bf16[128,896]{1,0:T(8,128)(2,1)S(1)} %arrived_block.3), channel_id=1, source_target_pairs={{1,0},{0,2},{2,3},{3,1},{5,4},{4,6},{6,7},{7,5},{9,8},{8,10},{10,1... | collective-permute-start | bytes 688136 | tf_op jit(solution)/shard_map/ppermute | solution.py:112
  18.6 9.8 %collective-permute-start.4 = (bf16[128,896]{1,0:T(8,128)(2,1)S(1)}, bf16[128,896]{1,0:T(8,128)(2,1)S(1)}, u32[]{:S(2)}, u32[]{:S(2)}) collective-permute-start(bf16[128,896]{1,0:T(8,128)(2,1)S(1)} %collective-permute-done.2.x_ref), channel_id=1, source_target_pairs={{1,0},{0,2},{2,3},{3,1},{5,4},{4,6},{6,7},{7,5},{9,8},{8,10},{10,1... | collective-permute-start | bytes 688136 | tf_op jit(solution)/shard_map/ppermute | solution.py:107
  23.9 7.7 %collective-permute-start.3 = (bf16[128,896]{1,0:T(8,128)(2,1)S(1)}, bf16[128,896]{1,0:T(8,128)(2,1)S(1)}, u32[]{:S(2)}, u32[]{:S(2)}) collective-permute-start(bf16[128,896]{1,0:T(8,128)(2,1)S(1)} %add_convert_fusion.2), channel_id=1, source_target_pairs={{1,0},{0,2},{2,3},{3,1},{5,4},{4,6},{6,7},{7,5},{9,8},{8,10},{10,1... | collective-permute-start | bytes 688136 | tf_op jit(solution)/shard_map/ppermute | solution.py:112
  31.6 6.6 %collective-permute-start.5 = (bf16[128,896]{1,0:T(8,128)(2,1)S(1)}, bf16[128,896]{1,0:T(8,128)(2,1)S(1)}, u32[]{:S(2)}, u32[]{:S(2)}) collective-permute-start(bf16[128,896]{1,0:T(8,128)(2,1)S(1)} %add_convert_fusion.1), channel_id=1, source_target_pairs={{1,0},{0,2},{2,3},{3,1},{5,4},{4,6},{6,7},{7,5},{9,8},{8,10},{10,1... | collective-permute-start | bytes 688136 | tf_op jit(solution)/shard_map/ppermute | solution.py:114

commit v2 on v1

--- a/solution.py
+++ b/solution.py
@@ -1,5 +1,3 @@
-import functools
-
 import jax
 import jax.numpy as jnp
 from jax import lax
@@ -95,24 +93,45 @@
     )(x, scale, *weights)
 
 
+def hop(block, route):
+    return lax.ppermute(block, "tensor", route)
+
+
+def add(arrived, part):
+    return (arrived.astype(jnp.float32) + part).astype(jnp.bfloat16)
+
+
+def line_of_four(tokens, own, scale, weights):
+    across = {distance: [(place, place ^ distance) for place in range(4)] for distance in (1, 2, 3)}
+    x_1 = hop(tokens, across[1])
+    x_3, own = lax.optimization_barrier((hop(tokens, across[3]), own))
+    part_1 = arrived_block(x_1, scale, weights, jnp.bfloat16)
+    x_2 = hop(x_3, across[1])
+    beside = hop(arrived_block(x_3, scale, weights, jnp.bfloat16), across[1])
+    part_2, part_1 = lax.optimization_barrier((arrived_block(x_2, scale, weights, jnp.float32), part_1))
+    from_neighbour = hop(part_1, across[1])
+    from_far = hop(add(beside, part_2), across[2])
+    return (own + from_neighbour.astype(jnp.float32) + from_far.astype(jnp.float32)).astype(jnp.bfloat16)
+
+
+def folded_ring(tokens, own, scale, weights, n):
+    order = list(range(0, n, 2)) + list(range(1, n, 2))[::-1]
+    route = [(order[k - 1], order[k]) for k in range(n)]
+    x, summed = tokens, None
+    for step in range(1, n):
+        x = hop(x, route)
+        part = arrived_block(x, scale, weights, jnp.bfloat16 if step == 1 else jnp.float32)
+        summed = part if step == 1 else add(hop(summed, route), part)
+    return add(hop(summed, route), own) if n > 1 else own.astype(jnp.bfloat16)
+
+
 def shards(tokens, smooth_scale, gate_weight, up_weight, down_weight):
     n = lax.axis_size("tensor")
-    ring = list(range(0, n, 2)) + list(range(1, n, 2))[::-1]
-    route = [(ring[k - 1], ring[k]) for k in range(n)]
-    send = functools.partial(lax.ppermute, axis_name="tensor", perm=route)
     scale = smooth_scale[None, :]
     own, weights = own_block(tokens, scale, (gate_weight, up_weight, down_weight))
-    x, summed = tokens, None
-    for hop in range(1, n):
-        x = send(x)
-        if hop == 1:
-            summed = arrived_block(x, scale, weights, jnp.bfloat16)
-        else:
-            part = arrived_block(x, scale, weights, jnp.float32)
-            summed = (send(summed).astype(jnp.float32) + part).astype(jnp.bfloat16)
-    if n > 1:
-        own = own + send(summed).astype(jnp.float32)
-    return own.astype(jnp.bfloat16)
+    if n == 4:
+        return line_of_four(tokens, own, scale, weights)
+    return folded_ring(tokens, own, scale, weights, n)
 
 
 def solution(mesh):

time: 39.2 us -> 39 us (level)
  starting transfers between devices: 17.1 us -> 11.4 us
  waiting for transfers between devices: 9.69 us -> 15.2 us
    ppermute x6, starting transfers between devices: 17.1 us -> 11.4 us  [hop(): return lax.ppermute(block, 'tensor', route)]
    ppermute x6, waiting for transfers between devices: 9.69 us -> 15.2 us  [hop(): return lax.ppermute(block, 'tensor', route)]
    convert_element_type x3 -> x2, other arithmetic: 0.81 us -> 0.8 us  [the longest x1 0.76 us: line_of_four(): (own + from_neighbour.astype(jnp.float32) + from_far.astype(jnp.float32))...]
where the time goes in v2:
time: 39 us; the launch traced here: 38.8 us
  waiting for transfers between devices  15.2 us (39%)
  starting transfers between devices  11.4 us (29%)
  Pallas kernels  9.75 us (25%)
  local copies, waits for them, and re-layouts  1.63 us (4%)
  other arithmetic  0.8 us (2%)
    ppermute x6, waiting for transfers between devices, hop(): return lax.ppermute(block, 'tensor', route)  15.2 us
    ppermute x6, starting transfers between devices, hop(): return lax.ppermute(block, 'tensor', route)  11.4 us
    pallas_call x3, Pallas kernels, arrived_block(): pl.pallas_call(arrived_kernel, out_shape=jax.ShapeDtypeStruct((rows, widt...  5.72 us
    pallas_call x1, Pallas kernels, own_block(): pl.pallas_call(own_kernel, out_shape=(jax.ShapeDtypeStruct((rows, width),...  4.03 us
    unnamed x2, local copies, waits for them, and re-layouts  0.94 us
  transfers between devices with their start and end apart: 6, of which 4 were waited for; matrix products, arithmetic and copies ran while one was open for 2% of the time, Pallas kernels for 25%

profile of v2, /device:TPU:0, one launch (start us, length us, event | category | flops | bytes accessed | tf_op | source)
XLA Modules:
  0.0 38.8 jit_solution(18031096790076264887)
XLA Ops:
  0.0 5.0 %collective-permute-start = (bf16[128,896]{1,0:T(8,128)(2,1)}, bf16[128,896]{1,0:T(8,128)(2,1)S(1)}, u32[]{:S(2)}, u32[]{:S(2)}) collective-permute-start(bf16[128,896]{1,0:T(8,128)(2,1)} %x_ref.1), channel_id=1, source_target_pairs={{0,3},{1,2},{2,1},{3,0},{4,7},{5,6},{6,5},{7,4},{8,11},{9,10},{10,... | collective-permute-start | bytes 688136 | tf_op jit(solution)/shard_map/ppermute | solution.py:97
  5.0 0.0 collective-permute-start.2
  5.1 0.7 %broadcast_in_dim.3.scale_ref = f32[1,896]{1,0:T(1,128)S(1)} reshape(f32[896]{0:T(1024)} %param.6) | data formatting | bytes 7168 | tf_op jit(solution)/shard_map/broadcast_in_dim | solution.py:130
  5.7 0.0 copy-start
  5.7 0.9 %copy-done = bf16[128,896]{1,0:T(8,128)(2,1)S(1)} copy-done((bf16[128,896]{1,0:T(8,128)(2,1)S(1)}, bf16[128,896]{1,0:T(8,128)(2,1)}, u32[]{:S(2)}) %copy-start) | copy-done | bytes 229400
  6.7 4.0 %own_block.1 = (f32[128,896]{1,0:T(8,128)S(1)}, bf16[1216,896]{1,0:T(8,128)(2,1)S(1)}, bf16[1216,896]{1,0:T(8,128)(2,1)S(1)}, bf16[1216,896]{1,0:T(8,128)(2,1)S(1)}) custom-call(bf16[128,896]{1,0:T(8,128)(2,1)S(1)} %copy-done, f32[1,896]{1,0:T(1,128)S(1)} %broadcast_in_dim.3.scale_ref, bf16[1216,896]{1,0:T(8,128)(2,1)} %gate_hbm.1, ...), custom_call_target="tpu_custom_call" | custom-call | flops 836763648 | bytes 6537216 | tf_op jit(solution)/shard_map/own_block/pallas_call | solution.py:68
  10.7 1.1 %collective-permute-done.x_ref = bf16[128,896]{1,0:T(8,128)(2,1)S(1)} collective-permute-done((bf16[128,896]{1,0:T(8,128)(2,1)}, bf16[128,896]{1,0:T(8,128)(2,1)S(1)}, u32[]{:S(2)}, u32[]{:S(2)}) %collective-permute-start) | collective-permute-done | bytes 229408 | tf_op jit(solution)/shard_map/ppermute | solution.py:97
  11.8 3.7 %collective-permute-start.1 = (bf16[128,896]{1,0:T(8,128)(2,1)S(1)}, bf16[128,896]{1,0:T(8,128)(2,1)S(1)}, u32[]{:S(2)}, u32[]{:S(2)}) collective-permute-start(bf16[128,896]{1,0:T(8,128)(2,1)S(1)} %collective-permute-done.x_ref), channel_id=1, source_target_pairs={{0,1},{1,0},{2,3},{3,2},{4,5},{5,4},{6,7},{7,6},{8,9},{9,8},{10,11... | collective-permute-start | bytes 688136 | tf_op jit(solution)/shard_map/ppermute | solution.py:97
  15.5 1.9 %arrived_block.5 = bf16[128,896]{1,0:T(8,128)(2,1)S(1)} custom-call(bf16[128,896]{1,0:T(8,128)(2,1)S(1)} %collective-permute-done.x_ref, f32[1,896]{1,0:T(1,128)S(1)} %broadcast_in_dim.3.scale_ref, bf16[1216,896]{1,0:T(8,128)(2,1)S(1)} %get-tuple-element.16.gate_ref, bf16[1216,896]{1,0:T(8,128)(2,1)S(1)} %get-tuple-element.17.up_ref, ...), custom_call_target="tpu_custom_call" | custom-call | flops 836763648 | bytes 6537216 | tf_op jit(solution)/shard_map/arrived_block/pallas_call | solution.py:84
  17.4 0.1 collective-permute-start.4
  17.5 0.0 collective-permute-done.2.x_ref
  17.5 1.9 %arrived_block.4 = bf16[128,896]{1,0:T(8,128)(2,1)S(1)} custom-call(bf16[128,896]{1,0:T(8,128)(2,1)S(1)} %collective-permute-done.2.x_ref, f32[1,896]{1,0:T(1,128)S(1)} %broadcast_in_dim.3.scale_ref, bf16[1216,896]{1,0:T(8,128)(2,1)S(1)} %get-tuple-element.16.gate_ref, bf16[1216,896]{1,0:T(8,128)(2,1)S(1)} %get-tuple-element.17.up_ref, ...), custom_call_target="tpu_custom_call" | custom-call | flops 836763648 | bytes 6537216 | tf_op jit(solution)/shard_map/arrived_block/pallas_call | solution.py:84
  19.4 2.6 %collective-permute-done.1.x_ref = bf16[128,896]{1,0:T(8,128)(2,1)S(1)} collective-permute-done((bf16[128,896]{1,0:T(8,128)(2,1)S(1)}, bf16[128,896]{1,0:T(8,128)(2,1)S(1)}, u32[]{:S(2)}, u32[]{:S(2)}) %collective-permute-start.1) | collective-permute-done | bytes 229408 | tf_op jit(solution)/shard_map/ppermute | solution.py:97
  22.0 1.9 %arrived_block.3 = f32[128,896]{1,0:T(8,128)S(1)} custom-call(bf16[128,896]{1,0:T(8,128)(2,1)S(1)} %collective-permute-done.1.x_ref, f32[1,896]{1,0:T(1,128)S(1)} %broadcast_in_dim.3.scale_ref, bf16[1216,896]{1,0:T(8,128)(2,1)S(1)} %get-tuple-element.16.gate_ref, bf16[1216,896]{1,0:T(8,128)(2,1)S(1)} %get-tuple-element.17.up_ref, ...), custom_call_target="tpu_custom_call" | custom-call | flops 836763648 | bytes 6537216 | tf_op jit(solution)/shard_map/arrived_block/pallas_call | solution.py:84
  23.9 1.8 %collective-permute-done.4 = bf16[128,896]{1,0:T(8,128)(2,1)S(1)} collective-permute-done((bf16[128,896]{1,0:T(8,128)(2,1)S(1)}, bf16[128,896]{1,0:T(8,128)(2,1)S(1)}, u32[]{:S(2)}, u32[]{:S(2)}) %collective-permute-start.4) | collective-permute-done | bytes 229408 | tf_op jit(solution)/shard_map/ppermute | solution.py:97
  25.8 2.2 %collective-permute-start.5 = (bf16[128,896]{1,0:T(8,128)(2,1)S(1)}, bf16[128,896]{1,0:T(8,128)(2,1)S(1)}, u32[]{:S(2)}, u32[]{:S(2)}) collective-permute-start(bf16[128,896]{1,0:T(8,128)(2,1)S(1)} %add_convert_fusion.1), channel_id=1, source_target_pairs={{0,2},{1,3},{2,0},{3,1},{4,6},{5,7},{6,4},{7,5},{8,10},{9,11},{10,... | collective-permute-start | bytes 688136 | tf_op jit(solution)/shard_map/ppermute | solution.py:97
  28.0 0.3 collective-permute-start.3
  28.3 9.8 %collective-permute-done.5 = bf16[128,896]{1,0:T(8,128)(2,1)S(1)} collective-permute-done((bf16[128,896]{1,0:T(8,128)(2,1)S(1)}, bf16[128,896]{1,0:T(8,128)(2,1)S(1)}, u32[]{:S(2)}, u32[]{:S(2)}) %collective-permute-start.5) | collective-permute-done | bytes 229408 | tf_op jit(solution)/shard_map/ppermute | solution.py:97
  38.1 0.0 collective-permute-done.3
  38.1 0.8 %add_convert_fusion = bf16[128,896]{1,0:T(8,128)(2,1)} fusion(bf16[128,896]{1,0:T(8,128)(2,1)S(1)} %collective-permute-done.5, f32[128,896]{1,0:T(8,128)S(1)} %get-tuple-element.14, bf16[128,896]{1,0:T(8,128)(2,1)S(1)} %collective-permute-done.3), kind=kLoop, calls=%fused_computation | loop fusion | flops 573440 | bytes 1146880 | tf_op jit(solution)/shard_map/convert_element_type | solution.py:114
  (1 shorter events, 0.0 us)
Async XLA Ops:
  0.0 11.8 %collective-permute-start = (bf16[128,896]{1,0:T(8,128)(2,1)}, bf16[128,896]{1,0:T(8,128)(2,1)S(1)}, u32[]{:S(2)}, u32[]{:S(2)}) collective-permute-start(bf16[128,896]{1,0:T(8,128)(2,1)} %x_ref.1), channel_id=1, source_target_pairs={{0,3},{1,2},{2,1},{3,0},{4,7},{5,6},{6,5},{7,4},{8,11},{9,10},{10,... | collective-permute-start | bytes 688136 | tf_op jit(solution)/shard_map/ppermute | solution.py:97
  5.0 12.4 %collective-permute-start.2 = (bf16[128,896]{1,0:T(8,128)(2,1)}, bf16[128,896]{1,0:T(8,128)(2,1)S(1)}, u32[]{:S(2)}, u32[]{:S(2)}) collective-permute-start(bf16[128,896]{1,0:T(8,128)(2,1)} %x_ref.1), channel_id=1, source_target_pairs={{0,1},{1,0},{2,3},{3,2},{4,5},{5,4},{6,7},{7,6},{8,9},{9,8},{10,11... | collective-permute-start | bytes 688136 | tf_op jit(solution)/shard_map/ppermute | solution.py:97
  5.7 0.9 %copy-start = (bf16[128,896]{1,0:T(8,128)(2,1)S(1)}, bf16[128,896]{1,0:T(8,128)(2,1)}, u32[]{:S(2)}) copy-start(bf16[128,896]{1,0:T(8,128)(2,1)} %x_ref.1) | copy-start | bytes 688132
  11.8 10.2 %collective-permute-start.1 = (bf16[128,896]{1,0:T(8,128)(2,1)S(1)}, bf16[128,896]{1,0:T(8,128)(2,1)S(1)}, u32[]{:S(2)}, u32[]{:S(2)}) collective-permute-start(bf16[128,896]{1,0:T(8,128)(2,1)S(1)} %collective-permute-done.x_ref), channel_id=1, source_target_pairs={{0,1},{1,0},{2,3},{3,2},{4,5},{5,4},{6,7},{7,6},{8,9},{9,8},{10,11... | collective-permute-start | bytes 688136 | tf_op jit(solution)/shard_map/ppermute | solution.py:97
  17.4 8.3 %collective-permute-start.4 = (bf16[128,896]{1,0:T(8,128)(2,1)S(1)}, bf16[128,896]{1,0:T(8,128)(2,1)S(1)}, u32[]{:S(2)}, u32[]{:S(2)}) collective-permute-start(bf16[128,896]{1,0:T(8,128)(2,1)S(1)} %arrived_block.5), channel_id=1, source_target_pairs={{0,1},{1,0},{2,3},{3,2},{4,5},{5,4},{6,7},{7,6},{8,9},{9,8},{10,11... | collective-permute-start | bytes 688136 | tf_op jit(solution)/shard_map/ppermute | solution.py:97
  25.8 12.3 %collective-permute-start.5 = (bf16[128,896]{1,0:T(8,128)(2,1)S(1)}, bf16[128,896]{1,0:T(8,128)(2,1)S(1)}, u32[]{:S(2)}, u32[]{:S(2)}) collective-permute-start(bf16[128,896]{1,0:T(8,128)(2,1)S(1)} %add_convert_fusion.1), channel_id=1, source_target_pairs={{0,2},{1,3},{2,0},{3,1},{4,6},{5,7},{6,4},{7,5},{8,10},{9,11},{10,... | collective-permute-start | bytes 688136 | tf_op jit(solution)/shard_map/ppermute | solution.py:97
  28.0 10.1 %collective-permute-start.3 = (bf16[128,896]{1,0:T(8,128)(2,1)S(1)}, bf16[128,896]{1,0:T(8,128)(2,1)S(1)}, u32[]{:S(2)}, u32[]{:S(2)}) collective-permute-start(bf16[128,896]{1,0:T(8,128)(2,1)S(1)} %arrived_block.4), channel_id=1, source_target_pairs={{0,1},{1,0},{2,3},{3,2},{4,5},{5,4},{6,7},{7,6},{8,9},{9,8},{10,11... | collective-permute-start | bytes 688136 | tf_op jit(solution)/shard_map/ppermute | solution.py:97

commit v3 on v2

--- a/solution.py
+++ b/solution.py
@@ -108,8 +108,8 @@
     part_1 = arrived_block(x_1, scale, weights, jnp.bfloat16)
     x_2 = hop(x_3, across[1])
     beside = hop(arrived_block(x_3, scale, weights, jnp.bfloat16), across[1])
-    part_2, part_1 = lax.optimization_barrier((arrived_block(x_2, scale, weights, jnp.float32), part_1))
     from_neighbour = hop(part_1, across[1])
+    part_2 = arrived_block(x_2, scale, weights, jnp.float32)
     from_far = hop(add(beside, part_2), across[2])
     return (own + from_neighbour.astype(jnp.float32) + from_far.astype(jnp.float32)).astype(jnp.bfloat16)
 

time: 39 us -> 39.2 us (level)
  starting transfers between devices: 11.4 us -> 14 us
  waiting for transfers between devices: 15.2 us -> 12.8 us
    ppermute x6, starting transfers between devices: 11.4 us -> 14 us  [hop(): return lax.ppermute(block, 'tensor', route)]
    ppermute x6, waiting for transfers between devices: 15.2 us -> 12.8 us  [hop(): return lax.ppermute(block, 'tensor', route)]
  transfers between devices with their start and end apart: 6 -> 6, of which waited for: 4 -> 5; matrix products, arithmetic and copies ran while one was open for 2% -> 2% of each run, Pallas kernels for 25% -> 25%
where the time goes in v3:
time: 39.2 us; the launch traced here: 39 us
  starting transfers between devices  14 us (36%)
  waiting for transfers between devices  12.8 us (33%)
  Pallas kernels  9.75 us (25%)
  local copies, waits for them, and re-layouts  1.63 us (4%)
  other arithmetic  0.8 us (2%)
    ppermute x6, starting transfers between devices, hop(): return lax.ppermute(block, 'tensor', route)  14 us
    ppermute x6, waiting for transfers between devices, hop(): return lax.ppermute(block, 'tensor', route)  12.8 us
    pallas_call x3, Pallas kernels, arrived_block(): pl.pallas_call(arrived_kernel, out_shape=jax.ShapeDtypeStruct((rows, widt...  5.72 us
    pallas_call x1, Pallas kernels, own_block(): pl.pallas_call(own_kernel, out_shape=(jax.ShapeDtypeStruct((rows, width),...  4.03 us
    unnamed x2, local copies, waits for them, and re-layouts  0.94 us
  transfers between devices with their start and end apart: 6, of which 5 were waited for; matrix products, arithmetic and copies ran while one was open for 2% of the time, Pallas kernels for 25%

profile of v3, /device:TPU:0, one launch (start us, length us, event | category | flops | bytes accessed | tf_op | source)
XLA Modules:
  0.0 39.0 jit_solution(8545727167848050566)
XLA Ops:
  0.0 5.0 %collective-permute-start = (bf16[128,896]{1,0:T(8,128)(2,1)}, bf16[128,896]{1,0:T(8,128)(2,1)S(1)}, u32[]{:S(2)}, u32[]{:S(2)}) collective-permute-start(bf16[128,896]{1,0:T(8,128)(2,1)} %x_ref.1), channel_id=1, source_target_pairs={{0,3},{1,2},{2,1},{3,0},{4,7},{5,6},{6,5},{7,4},{8,11},{9,10},{10,... | collective-permute-start | bytes 688136 | tf_op jit(solution)/shard_map/ppermute | solution.py:97
  5.0 0.0 collective-permute-start.1
  5.1 0.7 %broadcast_in_dim.3.scale_ref = f32[1,896]{1,0:T(1,128)S(1)} reshape(f32[896]{0:T(1024)} %param.6) | data formatting | bytes 7168 | tf_op jit(solution)/shard_map/broadcast_in_dim | solution.py:130
  5.7 0.0 copy-start
  5.7 0.9 %copy-done = bf16[128,896]{1,0:T(8,128)(2,1)S(1)} copy-done((bf16[128,896]{1,0:T(8,128)(2,1)S(1)}, bf16[128,896]{1,0:T(8,128)(2,1)}, u32[]{:S(2)}) %copy-start) | copy-done | bytes 229400
  6.7 4.0 %own_block.1 = (f32[128,896]{1,0:T(8,128)S(1)}, bf16[1216,896]{1,0:T(8,128)(2,1)S(1)}, bf16[1216,896]{1,0:T(8,128)(2,1)S(1)}, bf16[1216,896]{1,0:T(8,128)(2,1)S(1)}) custom-call(bf16[128,896]{1,0:T(8,128)(2,1)S(1)} %copy-done, f32[1,896]{1,0:T(1,128)S(1)} %broadcast_in_dim.3.scale_ref, bf16[1216,896]{1,0:T(8,128)(2,1)} %gate_hbm.1, ...), custom_call_target="tpu_custom_call" | custom-call | flops 836763648 | bytes 6537216 | tf_op jit(solution)/shard_map/own_block/pallas_call | solution.py:68
  10.7 1.1 %collective-permute-done.x_ref = bf16[128,896]{1,0:T(8,128)(2,1)S(1)} collective-permute-done((bf16[128,896]{1,0:T(8,128)(2,1)}, bf16[128,896]{1,0:T(8,128)(2,1)S(1)}, u32[]{:S(2)}, u32[]{:S(2)}) %collective-permute-start) | collective-permute-done | bytes 229408 | tf_op jit(solution)/shard_map/ppermute | solution.py:97
  11.8 3.7 %collective-permute-start.4 = (bf16[128,896]{1,0:T(8,128)(2,1)S(1)}, bf16[128,896]{1,0:T(8,128)(2,1)S(1)}, u32[]{:S(2)}, u32[]{:S(2)}) collective-permute-start(bf16[128,896]{1,0:T(8,128)(2,1)S(1)} %collective-permute-done.x_ref), channel_id=1, source_target_pairs={{0,1},{1,0},{2,3},{3,2},{4,5},{5,4},{6,7},{7,6},{8,9},{9,8},{10,11... | collective-permute-start | bytes 688136 | tf_op jit(solution)/shard_map/ppermute | solution.py:97
  15.5 1.9 %arrived_block.4 = bf16[128,896]{1,0:T(8,128)(2,1)S(1)} custom-call(bf16[128,896]{1,0:T(8,128)(2,1)S(1)} %collective-permute-done.x_ref, f32[1,896]{1,0:T(1,128)S(1)} %broadcast_in_dim.3.scale_ref, bf16[1216,896]{1,0:T(8,128)(2,1)S(1)} %get-tuple-element.13.gate_ref, bf16[1216,896]{1,0:T(8,128)(2,1)S(1)} %get-tuple-element.14.up_ref, ...), custom_call_target="tpu_custom_call" | custom-call | flops 836763648 | bytes 6537216 | tf_op jit(solution)/shard_map/arrived_block/pallas_call | solution.py:84
  17.4 0.1 collective-permute-start.3
  17.5 0.0 collective-permute-done.1.x_ref
  17.5 1.9 %arrived_block.3 = bf16[128,896]{1,0:T(8,128)(2,1)S(1)} custom-call(bf16[128,896]{1,0:T(8,128)(2,1)S(1)} %collective-permute-done.1.x_ref, f32[1,896]{1,0:T(1,128)S(1)} %broadcast_in_dim.3.scale_ref, bf16[1216,896]{1,0:T(8,128)(2,1)S(1)} %get-tuple-element.13.gate_ref, bf16[1216,896]{1,0:T(8,128)(2,1)S(1)} %get-tuple-element.14.up_ref, ...), custom_call_target="tpu_custom_call" | custom-call | flops 836763648 | bytes 6537216 | tf_op jit(solution)/shard_map/arrived_block/pallas_call | solution.py:84
  19.4 2.1 %collective-permute-start.2 = (bf16[128,896]{1,0:T(8,128)(2,1)S(1)}, bf16[128,896]{1,0:T(8,128)(2,1)S(1)}, u32[]{:S(2)}, u32[]{:S(2)}) collective-permute-start(bf16[128,896]{1,0:T(8,128)(2,1)S(1)} %arrived_block.3), channel_id=1, source_target_pairs={{0,1},{1,0},{2,3},{3,2},{4,5},{5,4},{6,7},{7,6},{8,9},{9,8},{10,11... | collective-permute-start | bytes 688136 | tf_op jit(solution)/shard_map/ppermute | solution.py:97
  21.5 0.5 %collective-permute-done.4.x_ref = bf16[128,896]{1,0:T(8,128)(2,1)S(1)} collective-permute-done((bf16[128,896]{1,0:T(8,128)(2,1)S(1)}, bf16[128,896]{1,0:T(8,128)(2,1)S(1)}, u32[]{:S(2)}, u32[]{:S(2)}) %collective-permute-start.4) | collective-permute-done | bytes 229408 | tf_op jit(solution)/shard_map/ppermute | solution.py:97
  22.0 1.9 %arrived_block.5 = f32[128,896]{1,0:T(8,128)S(1)} custom-call(bf16[128,896]{1,0:T(8,128)(2,1)S(1)} %collective-permute-done.4.x_ref, f32[1,896]{1,0:T(1,128)S(1)} %broadcast_in_dim.3.scale_ref, bf16[1216,896]{1,0:T(8,128)(2,1)S(1)} %get-tuple-element.13.gate_ref, bf16[1216,896]{1,0:T(8,128)(2,1)S(1)} %get-tuple-element.14.up_ref, ...), custom_call_target="tpu_custom_call" | custom-call | flops 836763648 | bytes 6537216 | tf_op jit(solution)/shard_map/arrived_block/pallas_call | solution.py:84
  23.9 3.0 %collective-permute-done.3 = bf16[128,896]{1,0:T(8,128)(2,1)S(1)} collective-permute-done((bf16[128,896]{1,0:T(8,128)(2,1)S(1)}, bf16[128,896]{1,0:T(8,128)(2,1)S(1)}, u32[]{:S(2)}, u32[]{:S(2)}) %collective-permute-start.3) | collective-permute-done | bytes 229408 | tf_op jit(solution)/shard_map/ppermute | solution.py:97
  27.0 3.1 %collective-permute-start.5 = (bf16[128,896]{1,0:T(8,128)(2,1)S(1)}, bf16[128,896]{1,0:T(8,128)(2,1)S(1)}, u32[]{:S(2)}, u32[]{:S(2)}) collective-permute-start(bf16[128,896]{1,0:T(8,128)(2,1)S(1)} %add_convert_fusion.1), channel_id=1, source_target_pairs={{0,2},{1,3},{2,0},{3,1},{4,6},{5,7},{6,4},{7,5},{8,10},{9,11},{10,... | collective-permute-start | bytes 688136 | tf_op jit(solution)/shard_map/ppermute | solution.py:97
  30.1 4.5 %collective-permute-done.2 = bf16[128,896]{1,0:T(8,128)(2,1)S(1)} collective-permute-done((bf16[128,896]{1,0:T(8,128)(2,1)S(1)}, bf16[128,896]{1,0:T(8,128)(2,1)S(1)}, u32[]{:S(2)}, u32[]{:S(2)}) %collective-permute-start.2) | collective-permute-done | bytes 229408 | tf_op jit(solution)/shard_map/ppermute | solution.py:97
  34.5 3.7 %collective-permute-done.5 = bf16[128,896]{1,0:T(8,128)(2,1)S(1)} collective-permute-done((bf16[128,896]{1,0:T(8,128)(2,1)S(1)}, bf16[128,896]{1,0:T(8,128)(2,1)S(1)}, u32[]{:S(2)}, u32[]{:S(2)}) %collective-permute-start.5) | collective-permute-done | bytes 229408 | tf_op jit(solution)/shard_map/ppermute | solution.py:97
  38.3 0.8 %add_convert_fusion = bf16[128,896]{1,0:T(8,128)(2,1)} fusion(bf16[128,896]{1,0:T(8,128)(2,1)S(1)} %collective-permute-done.5, f32[128,896]{1,0:T(8,128)S(1)} %get-tuple-element.12, bf16[128,896]{1,0:T(8,128)(2,1)S(1)} %collective-permute-done.2), kind=kLoop, calls=%fused_computation | loop fusion | flops 573440 | bytes 1146880 | tf_op jit(solution)/shard_map/convert_element_type | solution.py:114
  (1 shorter events, 0.0 us)
Async XLA Ops:
  0.0 11.8 %collective-permute-start = (bf16[128,896]{1,0:T(8,128)(2,1)}, bf16[128,896]{1,0:T(8,128)(2,1)S(1)}, u32[]{:S(2)}, u32[]{:S(2)}) collective-permute-start(bf16[128,896]{1,0:T(8,128)(2,1)} %x_ref.1), channel_id=1, source_target_pairs={{0,3},{1,2},{2,1},{3,0},{4,7},{5,6},{6,5},{7,4},{8,11},{9,10},{10,... | collective-permute-start | bytes 688136 | tf_op jit(solution)/shard_map/ppermute | solution.py:97
  5.0 12.4 %collective-permute-start.1 = (bf16[128,896]{1,0:T(8,128)(2,1)}, bf16[128,896]{1,0:T(8,128)(2,1)S(1)}, u32[]{:S(2)}, u32[]{:S(2)}) collective-permute-start(bf16[128,896]{1,0:T(8,128)(2,1)} %x_ref.1), channel_id=1, source_target_pairs={{0,1},{1,0},{2,3},{3,2},{4,5},{5,4},{6,7},{7,6},{8,9},{9,8},{10,11... | collective-permute-start | bytes 688136 | tf_op jit(solution)/shard_map/ppermute | solution.py:97
  5.7 0.9 %copy-start = (bf16[128,896]{1,0:T(8,128)(2,1)S(1)}, bf16[128,896]{1,0:T(8,128)(2,1)}, u32[]{:S(2)}) copy-start(bf16[128,896]{1,0:T(8,128)(2,1)} %x_ref.1) | copy-start | bytes 688132
  11.8 10.2 %collective-permute-start.4 = (bf16[128,896]{1,0:T(8,128)(2,1)S(1)}, bf16[128,896]{1,0:T(8,128)(2,1)S(1)}, u32[]{:S(2)}, u32[]{:S(2)}) collective-permute-start(bf16[128,896]{1,0:T(8,128)(2,1)S(1)} %collective-permute-done.x_ref), channel_id=1, source_target_pairs={{0,1},{1,0},{2,3},{3,2},{4,5},{5,4},{6,7},{7,6},{8,9},{9,8},{10,11... | collective-permute-start | bytes 688136 | tf_op jit(solution)/shard_map/ppermute | solution.py:97
  17.4 9.5 %collective-permute-start.3 = (bf16[128,896]{1,0:T(8,128)(2,1)S(1)}, bf16[128,896]{1,0:T(8,128)(2,1)S(1)}, u32[]{:S(2)}, u32[]{:S(2)}) collective-permute-start(bf16[128,896]{1,0:T(8,128)(2,1)S(1)} %arrived_block.4), channel_id=1, source_target_pairs={{0,1},{1,0},{2,3},{3,2},{4,5},{5,4},{6,7},{7,6},{8,9},{9,8},{10,11... | collective-permute-start | bytes 688136 | tf_op jit(solution)/shard_map/ppermute | solution.py:97
  19.4 15.1 %collective-permute-start.2 = (bf16[128,896]{1,0:T(8,128)(2,1)S(1)}, bf16[128,896]{1,0:T(8,128)(2,1)S(1)}, u32[]{:S(2)}, u32[]{:S(2)}) collective-permute-start(bf16[128,896]{1,0:T(8,128)(2,1)S(1)} %arrived_block.3), channel_id=1, source_target_pairs={{0,1},{1,0},{2,3},{3,2},{4,5},{5,4},{6,7},{7,6},{8,9},{9,8},{10,11... | collective-permute-start | bytes 688136 | tf_op jit(solution)/shard_map/ppermute | solution.py:97
  27.0 11.3 %collective-permute-start.5 = (bf16[128,896]{1,0:T(8,128)(2,1)S(1)}, bf16[128,896]{1,0:T(8,128)(2,1)S(1)}, u32[]{:S(2)}, u32[]{:S(2)}) collective-permute-start(bf16[128,896]{1,0:T(8,128)(2,1)S(1)} %add_convert_fusion.1), channel_id=1, source_target_pairs={{0,2},{1,3},{2,0},{3,1},{4,6},{5,7},{6,4},{7,5},{8,10},{9,11},{10,... | collective-permute-start | bytes 688136 | tf_op jit(solution)/shard_map/ppermute | solution.py:97

commit v4 on v3

--- a/solution.py
+++ b/solution.py
@@ -104,13 +104,13 @@
 def line_of_four(tokens, own, scale, weights):
     across = {distance: [(place, place ^ distance) for place in range(4)] for distance in (1, 2, 3)}
     x_1 = hop(tokens, across[1])
-    x_3, own = lax.optimization_barrier((hop(tokens, across[3]), own))
+    x_2, own = lax.optimization_barrier((hop(tokens, across[2]), own))
     part_1 = arrived_block(x_1, scale, weights, jnp.bfloat16)
-    x_2 = hop(x_3, across[1])
-    beside = hop(arrived_block(x_3, scale, weights, jnp.bfloat16), across[1])
+    x_3 = hop(x_2, across[1])
+    beside = hop(arrived_block(x_2, scale, weights, jnp.bfloat16), across[1])
     from_neighbour = hop(part_1, across[1])
-    part_2 = arrived_block(x_2, scale, weights, jnp.float32)
-    from_far = hop(add(beside, part_2), across[2])
+    part_3 = arrived_block(x_3, scale, weights, jnp.float32)
+    from_far = hop(add(beside, part_3), across[3])
     return (own + from_neighbour.astype(jnp.float32) + from_far.astype(jnp.float32)).astype(jnp.bfloat16)
 
 

time: 39.2 us -> 39.9 us (1.018)
  waiting for transfers between devices: 12.8 us -> 15.4 us
  starting transfers between devices: 14 us -> 12.1 us
    ppermute x6, waiting for transfers between devices: 12.8 us -> 15.4 us  [hop(): return lax.ppermute(block, 'tensor', route)]
    ppermute x6, starting transfers between devices: 14 us -> 12.1 us  [hop(): return lax.ppermute(block, 'tensor', route)]
  transfers between devices with their start and end apart: 6 -> 6, of which waited for: 5 -> 4; matrix products, arithmetic and copies ran while one was open for 2% -> 2% of each run, Pallas kernels for 25% -> 25%
where the time goes in v4:
time: 39.9 us; the launch traced here: 39.7 us
  waiting for transfers between devices  15.4 us (39%)
  starting transfers between devices  12.1 us (30%)
  Pallas kernels  9.76 us (24%)
  local copies, waits for them, and re-layouts  1.63 us (4%)
  other arithmetic  0.8 us (2%)
    ppermute x6, waiting for transfers between devices, hop(): return lax.ppermute(block, 'tensor', route)  15.4 us
    ppermute x6, starting transfers between devices, hop(): return lax.ppermute(block, 'tensor', route)  12.1 us
    pallas_call x3, Pallas kernels, arrived_block(): pl.pallas_call(arrived_kernel, out_shape=jax.ShapeDtypeStruct((rows, widt...  5.72 us
    pallas_call x1, Pallas kernels, own_block(): pl.pallas_call(own_kernel, out_shape=(jax.ShapeDtypeStruct((rows, width),...  4.04 us
    unnamed x2, local copies, waits for them, and re-layouts  0.94 us
  transfers between devices with their start and end apart: 6, of which 4 were waited for; matrix products, arithmetic and copies ran while one was open for 2% of the time, Pallas kernels for 25%

profile of v4, /device:TPU:0, one launch (start us, length us, event | category | flops | bytes accessed | tf_op | source)
XLA Modules:
  0.0 39.7 jit_solution(459204130285807888)
XLA Ops:
  0.0 4.0 %collective-permute-start = (bf16[128,896]{1,0:T(8,128)(2,1)}, bf16[128,896]{1,0:T(8,128)(2,1)S(1)}, u32[]{:S(2)}, u32[]{:S(2)}) collective-permute-start(bf16[128,896]{1,0:T(8,128)(2,1)} %x_ref.1), channel_id=1, source_target_pairs={{0,2},{1,3},{2,0},{3,1},{4,6},{5,7},{6,4},{7,5},{8,10},{9,11},{10,... | collective-permute-start | bytes 688136 | tf_op jit(solution)/shard_map/ppermute | solution.py:97
  4.0 1.6 %collective-permute-start.1 = (bf16[128,896]{1,0:T(8,128)(2,1)}, bf16[128,896]{1,0:T(8,128)(2,1)S(1)}, u32[]{:S(2)}, u32[]{:S(2)}) collective-permute-start(bf16[128,896]{1,0:T(8,128)(2,1)} %x_ref.1), channel_id=1, source_target_pairs={{0,1},{1,0},{2,3},{3,2},{4,5},{5,4},{6,7},{7,6},{8,9},{9,8},{10,11... | collective-permute-start | bytes 688136 | tf_op jit(solution)/shard_map/ppermute | solution.py:97
  5.6 0.7 %broadcast_in_dim.3.scale_ref = f32[1,896]{1,0:T(1,128)S(1)} reshape(f32[896]{0:T(1024)} %param.6) | data formatting | bytes 7168 | tf_op jit(solution)/shard_map/broadcast_in_dim | solution.py:130
  6.3 0.0 copy-start
  6.3 0.9 %copy-done = bf16[128,896]{1,0:T(8,128)(2,1)S(1)} copy-done((bf16[128,896]{1,0:T(8,128)(2,1)S(1)}, bf16[128,896]{1,0:T(8,128)(2,1)}, u32[]{:S(2)}) %copy-start) | copy-done | bytes 229400
  7.2 4.0 %own_block.1 = (f32[128,896]{1,0:T(8,128)S(1)}, bf16[1216,896]{1,0:T(8,128)(2,1)S(1)}, bf16[1216,896]{1,0:T(8,128)(2,1)S(1)}, bf16[1216,896]{1,0:T(8,128)(2,1)S(1)}) custom-call(bf16[128,896]{1,0:T(8,128)(2,1)S(1)} %copy-done, f32[1,896]{1,0:T(1,128)S(1)} %broadcast_in_dim.3.scale_ref, bf16[1216,896]{1,0:T(8,128)(2,1)} %gate_hbm.1, ...), custom_call_target="tpu_custom_call" | custom-call | flops 836763648 | bytes 6537216 | tf_op jit(solution)/shard_map/own_block/pallas_call | solution.py:68
  11.3 3.6 %collective-permute-done.x_ref = bf16[128,896]{1,0:T(8,128)(2,1)S(1)} collective-permute-done((bf16[128,896]{1,0:T(8,128)(2,1)}, bf16[128,896]{1,0:T(8,128)(2,1)S(1)}, u32[]{:S(2)}, u32[]{:S(2)}) %collective-permute-start) | collective-permute-done | bytes 229408 | tf_op jit(solution)/shard_map/ppermute | solution.py:97
  14.9 0.7 %collective-permute-start.4 = (bf16[128,896]{1,0:T(8,128)(2,1)S(1)}, bf16[128,896]{1,0:T(8,128)(2,1)S(1)}, u32[]{:S(2)}, u32[]{:S(2)}) collective-permute-start(bf16[128,896]{1,0:T(8,128)(2,1)S(1)} %collective-permute-done.x_ref), channel_id=1, source_target_pairs={{0,1},{1,0},{2,3},{3,2},{4,5},{5,4},{6,7},{7,6},{8,9},{9,8},{10,11... | collective-permute-start | bytes 688136 | tf_op jit(solution)/shard_map/ppermute | solution.py:97
  15.6 1.9 %arrived_block.4 = bf16[128,896]{1,0:T(8,128)(2,1)S(1)} custom-call(bf16[128,896]{1,0:T(8,128)(2,1)S(1)} %collective-permute-done.x_ref, f32[1,896]{1,0:T(1,128)S(1)} %broadcast_in_dim.3.scale_ref, bf16[1216,896]{1,0:T(8,128)(2,1)S(1)} %get-tuple-element.13.gate_ref, bf16[1216,896]{1,0:T(8,128)(2,1)S(1)} %get-tuple-element.14.up_ref, ...), custom_call_target="tpu_custom_call" | custom-call | flops 836763648 | bytes 6537216 | tf_op jit(solution)/shard_map/arrived_block/pallas_call | solution.py:84
  17.5 1.4 %collective-permute-start.3 = (bf16[128,896]{1,0:T(8,128)(2,1)S(1)}, bf16[128,896]{1,0:T(8,128)(2,1)S(1)}, u32[]{:S(2)}, u32[]{:S(2)}) collective-permute-start(bf16[128,896]{1,0:T(8,128)(2,1)S(1)} %arrived_block.4), channel_id=1, source_target_pairs={{0,1},{1,0},{2,3},{3,2},{4,5},{5,4},{6,7},{7,6},{8,9},{9,8},{10,11... | collective-permute-start | bytes 688136 | tf_op jit(solution)/shard_map/ppermute | solution.py:97
  18.9 0.0 collective-permute-done.1.x_ref
  18.9 1.9 %arrived_block.3 = bf16[128,896]{1,0:T(8,128)(2,1)S(1)} custom-call(bf16[128,896]{1,0:T(8,128)(2,1)S(1)} %collective-permute-done.1.x_ref, f32[1,896]{1,0:T(1,128)S(1)} %broadcast_in_dim.3.scale_ref, bf16[1216,896]{1,0:T(8,128)(2,1)S(1)} %get-tuple-element.13.gate_ref, bf16[1216,896]{1,0:T(8,128)(2,1)S(1)} %get-tuple-element.14.up_ref, ...), custom_call_target="tpu_custom_call" | custom-call | flops 836763648 | bytes 6537216 | tf_op jit(solution)/shard_map/arrived_block/pallas_call | solution.py:84
  20.8 0.8 %collective-permute-start.2 = (bf16[128,896]{1,0:T(8,128)(2,1)S(1)}, bf16[128,896]{1,0:T(8,128)(2,1)S(1)}, u32[]{:S(2)}, u32[]{:S(2)}) collective-permute-start(bf16[128,896]{1,0:T(8,128)(2,1)S(1)} %arrived_block.3), channel_id=1, source_target_pairs={{0,1},{1,0},{2,3},{3,2},{4,5},{5,4},{6,7},{7,6},{8,9},{9,8},{10,11... | collective-permute-start | bytes 688136 | tf_op jit(solution)/shard_map/ppermute | solution.py:97
  21.6 1.7 %collective-permute-done.4.x_ref = bf16[128,896]{1,0:T(8,128)(2,1)S(1)} collective-permute-done((bf16[128,896]{1,0:T(8,128)(2,1)S(1)}, bf16[128,896]{1,0:T(8,128)(2,1)S(1)}, u32[]{:S(2)}, u32[]{:S(2)}) %collective-permute-start.4) | collective-permute-done | bytes 229408 | tf_op jit(solution)/shard_map/ppermute | solution.py:97
  23.2 1.9 %arrived_block.5 = f32[128,896]{1,0:T(8,128)S(1)} custom-call(bf16[128,896]{1,0:T(8,128)(2,1)S(1)} %collective-permute-done.4.x_ref, f32[1,896]{1,0:T(1,128)S(1)} %broadcast_in_dim.3.scale_ref, bf16[1216,896]{1,0:T(8,128)(2,1)S(1)} %get-tuple-element.13.gate_ref, bf16[1216,896]{1,0:T(8,128)(2,1)S(1)} %get-tuple-element.14.up_ref, ...), custom_call_target="tpu_custom_call" | custom-call | flops 836763648 | bytes 6537216 | tf_op jit(solution)/shard_map/arrived_block/pallas_call | solution.py:84
  25.1 3.0 %collective-permute-done.3 = bf16[128,896]{1,0:T(8,128)(2,1)S(1)} collective-permute-done((bf16[128,896]{1,0:T(8,128)(2,1)S(1)}, bf16[128,896]{1,0:T(8,128)(2,1)S(1)}, u32[]{:S(2)}, u32[]{:S(2)}) %collective-permute-start.3) | collective-permute-done | bytes 229408 | tf_op jit(solution)/shard_map/ppermute | solution.py:97
  28.2 3.6 %collective-permute-start.5 = (bf16[128,896]{1,0:T(8,128)(2,1)S(1)}, bf16[128,896]{1,0:T(8,128)(2,1)S(1)}, u32[]{:S(2)}, u32[]{:S(2)}) collective-permute-start(bf16[128,896]{1,0:T(8,128)(2,1)S(1)} %add_convert_fusion.1), channel_id=1, source_target_pairs={{0,3},{1,2},{2,1},{3,0},{4,7},{5,6},{6,5},{7,4},{8,11},{9,10},{10,... | collective-permute-start | bytes 688136 | tf_op jit(solution)/shard_map/ppermute | solution.py:97
  31.8 0.0 collective-permute-done.2
  31.8 7.1 %collective-permute-done.5 = bf16[128,896]{1,0:T(8,128)(2,1)S(1)} collective-permute-done((bf16[128,896]{1,0:T(8,128)(2,1)S(1)}, bf16[128,896]{1,0:T(8,128)(2,1)S(1)}, u32[]{:S(2)}, u32[]{:S(2)}) %collective-permute-start.5) | collective-permute-done | bytes 229408 | tf_op jit(solution)/shard_map/ppermute | solution.py:97
  38.9 0.8 %add_convert_fusion = bf16[128,896]{1,0:T(8,128)(2,1)} fusion(bf16[128,896]{1,0:T(8,128)(2,1)S(1)} %collective-permute-done.5, f32[128,896]{1,0:T(8,128)S(1)} %get-tuple-element.12, bf16[128,896]{1,0:T(8,128)(2,1)S(1)} %collective-permute-done.2), kind=kLoop, calls=%fused_computation | loop fusion | flops 573440 | bytes 1146880 | tf_op jit(solution)/shard_map/convert_element_type | solution.py:114
  (1 shorter events, 0.0 us)
Async XLA Ops:
  0.0 14.9 %collective-permute-start = (bf16[128,896]{1,0:T(8,128)(2,1)}, bf16[128,896]{1,0:T(8,128)(2,1)S(1)}, u32[]{:S(2)}, u32[]{:S(2)}) collective-permute-start(bf16[128,896]{1,0:T(8,128)(2,1)} %x_ref.1), channel_id=1, source_target_pairs={{0,2},{1,3},{2,0},{3,1},{4,6},{5,7},{6,4},{7,5},{8,10},{9,11},{10,... | collective-permute-start | bytes 688136 | tf_op jit(solution)/shard_map/ppermute | solution.py:97
  4.0 14.9 %collective-permute-start.1 = (bf16[128,896]{1,0:T(8,128)(2,1)}, bf16[128,896]{1,0:T(8,128)(2,1)S(1)}, u32[]{:S(2)}, u32[]{:S(2)}) collective-permute-start(bf16[128,896]{1,0:T(8,128)(2,1)} %x_ref.1), channel_id=1, source_target_pairs={{0,1},{1,0},{2,3},{3,2},{4,5},{5,4},{6,7},{7,6},{8,9},{9,8},{10,11... | collective-permute-start | bytes 688136 | tf_op jit(solution)/shard_map/ppermute | solution.py:97
  6.3 0.9 %copy-start = (bf16[128,896]{1,0:T(8,128)(2,1)S(1)}, bf16[128,896]{1,0:T(8,128)(2,1)}, u32[]{:S(2)}) copy-start(bf16[128,896]{1,0:T(8,128)(2,1)} %x_ref.1) | copy-start | bytes 688132
  14.9 8.4 %collective-permute-start.4 = (bf16[128,896]{1,0:T(8,128)(2,1)S(1)}, bf16[128,896]{1,0:T(8,128)(2,1)S(1)}, u32[]{:S(2)}, u32[]{:S(2)}) collective-permute-start(bf16[128,896]{1,0:T(8,128)(2,1)S(1)} %collective-permute-done.x_ref), channel_id=1, source_target_pairs={{0,1},{1,0},{2,3},{3,2},{4,5},{5,4},{6,7},{7,6},{8,9},{9,8},{10,11... | collective-permute-start | bytes 688136 | tf_op jit(solution)/shard_map/ppermute | solution.py:97
  17.5 10.6 %collective-permute-start.3 = (bf16[128,896]{1,0:T(8,128)(2,1)S(1)}, bf16[128,896]{1,0:T(8,128)(2,1)S(1)}, u32[]{:S(2)}, u32[]{:S(2)}) collective-permute-start(bf16[128,896]{1,0:T(8,128)(2,1)S(1)} %arrived_block.4), channel_id=1, source_target_pairs={{0,1},{1,0},{2,3},{3,2},{4,5},{5,4},{6,7},{7,6},{8,9},{9,8},{10,11... | collective-permute-start | bytes 688136 | tf_op jit(solution)/shard_map/ppermute | solution.py:97
  20.8 11.0 %collective-permute-start.2 = (bf16[128,896]{1,0:T(8,128)(2,1)S(1)}, bf16[128,896]{1,0:T(8,128)(2,1)S(1)}, u32[]{:S(2)}, u32[]{:S(2)}) collective-permute-start(bf16[128,896]{1,0:T(8,128)(2,1)S(1)} %arrived_block.3), channel_id=1, source_target_pairs={{0,1},{1,0},{2,3},{3,2},{4,5},{5,4},{6,7},{7,6},{8,9},{9,8},{10,11... | collective-permute-start | bytes 688136 | tf_op jit(solution)/shard_map/ppermute | solution.py:97
  28.2 10.7 %collective-permute-start.5 = (bf16[128,896]{1,0:T(8,128)(2,1)S(1)}, bf16[128,896]{1,0:T(8,128)(2,1)S(1)}, u32[]{:S(2)}, u32[]{:S(2)}) collective-permute-start(bf16[128,896]{1,0:T(8,128)(2,1)S(1)} %add_convert_fusion.1), channel_id=1, source_target_pairs={{0,3},{1,2},{2,1},{3,0},{4,7},{5,6},{6,5},{7,4},{8,11},{9,10},{10,... | collective-permute-start | bytes 688136 | tf_op jit(solution)/shard_map/ppermute | solution.py:97

commit v5 on v3

--- a/solution.py
+++ b/solution.py
@@ -105,13 +105,11 @@
     across = {distance: [(place, place ^ distance) for place in range(4)] for distance in (1, 2, 3)}
     x_1 = hop(tokens, across[1])
     x_3, own = lax.optimization_barrier((hop(tokens, across[3]), own))
-    part_1 = arrived_block(x_1, scale, weights, jnp.bfloat16)
     x_2 = hop(x_3, across[1])
-    beside = hop(arrived_block(x_3, scale, weights, jnp.bfloat16), across[1])
-    from_neighbour = hop(part_1, across[1])
-    part_2 = arrived_block(x_2, scale, weights, jnp.float32)
-    from_far = hop(add(beside, part_2), across[2])
-    return (own + from_neighbour.astype(jnp.float32) + from_far.astype(jnp.float32)).astype(jnp.bfloat16)
+    own = own.astype(jnp.float32)
+    for x, distance in ((x_3, 3), (x_1, 1), (x_2, 2)):
+        own = own + hop(arrived_block(x, scale, weights, jnp.bfloat16), across[distance]).astype(jnp.float32)
+    return own.astype(jnp.bfloat16)
 
 
 def folded_ring(tokens, own, scale, weights, n):

time: 39.2 us -> 39.3 us (level)
    convert_element_type x2 -> x1, other arithmetic: 0.8 us -> 0.79 us  [line_of_four(): return own.astype(jnp.bfloat16)]
  transfers between devices with their start and end apart: 6 -> 6, of which waited for: 5 -> 4; matrix products, arithmetic and copies ran while one was open for 2% -> 2% of each run, Pallas kernels for 25% -> 25%
where the time goes in v5:
time: 39.3 us; the launch traced here: 39.1 us
  starting transfers between devices  14.1 us (36%)
  waiting for transfers between devices  12.8 us (33%)
  Pallas kernels  9.75 us (25%)
  local copies, waits for them, and re-layouts  1.63 us (4%)
  other arithmetic  0.79 us (2%)
    ppermute x6, starting transfers between devices, hop(): return lax.ppermute(block, 'tensor', route)  14.1 us
    ppermute x6, waiting for transfers between devices, hop(): return lax.ppermute(block, 'tensor', route)  12.8 us
    pallas_call x3, Pallas kernels, arrived_block(): pl.pallas_call(arrived_kernel, out_shape=jax.ShapeDtypeStruct((rows, widt...  5.72 us
    pallas_call x1, Pallas kernels, own_block(): pl.pallas_call(own_kernel, out_shape=(jax.ShapeDtypeStruct((rows, width),...  4.03 us
    unnamed x2, local copies, waits for them, and re-layouts  0.94 us
    convert_element_type x1, other arithmetic, line_of_four(): return own.astype(jnp.bfloat16)  0.79 us
  transfers between devices with their start and end apart: 6, of which 4 were waited for; matrix products, arithmetic and copies ran while one was open for 2% of the time, Pallas kernels for 25%

profile of v5, /device:TPU:0, one launch (start us, length us, event | category | flops | bytes accessed | tf_op | source)
XLA Modules:
  0.0 39.1 jit_solution(17096699851145256710)
XLA Ops:
  0.0 5.0 %collective-permute-start = (bf16[128,896]{1,0:T(8,128)(2,1)}, bf16[128,896]{1,0:T(8,128)(2,1)S(1)}, u32[]{:S(2)}, u32[]{:S(2)}) collective-permute-start(bf16[128,896]{1,0:T(8,128)(2,1)} %x_ref.1), channel_id=1, source_target_pairs={{0,3},{1,2},{2,1},{3,0},{4,7},{5,6},{6,5},{7,4},{8,11},{9,10},{10,... | collective-permute-start | bytes 688136 | tf_op jit(solution)/shard_map/ppermute | solution.py:97
  5.0 0.0 collective-permute-start.2
  5.1 0.7 %broadcast_in_dim.3.scale_ref = f32[1,896]{1,0:T(1,128)S(1)} reshape(f32[896]{0:T(1024)} %param.6) | data formatting | bytes 7168 | tf_op jit(solution)/shard_map/broadcast_in_dim | solution.py:128
  5.7 0.0 copy-start
  5.7 0.9 %copy-done = bf16[128,896]{1,0:T(8,128)(2,1)S(1)} copy-done((bf16[128,896]{1,0:T(8,128)(2,1)S(1)}, bf16[128,896]{1,0:T(8,128)(2,1)}, u32[]{:S(2)}) %copy-start) | copy-done | bytes 229400
  6.7 4.0 %own_block.1 = (f32[128,896]{1,0:T(8,128)S(1)}, bf16[1216,896]{1,0:T(8,128)(2,1)S(1)}, bf16[1216,896]{1,0:T(8,128)(2,1)S(1)}, bf16[1216,896]{1,0:T(8,128)(2,1)S(1)}) custom-call(bf16[128,896]{1,0:T(8,128)(2,1)S(1)} %copy-done, f32[1,896]{1,0:T(1,128)S(1)} %broadcast_in_dim.3.scale_ref, bf16[1216,896]{1,0:T(8,128)(2,1)} %gate_hbm.1, ...), custom_call_target="tpu_custom_call" | custom-call | flops 836763648 | bytes 6537216 | tf_op jit(solution)/shard_map/own_block/pallas_call | solution.py:68
  10.7 1.1 %collective-permute-done.x_ref = bf16[128,896]{1,0:T(8,128)(2,1)S(1)} collective-permute-done((bf16[128,896]{1,0:T(8,128)(2,1)}, bf16[128,896]{1,0:T(8,128)(2,1)S(1)}, u32[]{:S(2)}, u32[]{:S(2)}) %collective-permute-start) | collective-permute-done | bytes 229408 | tf_op jit(solution)/shard_map/ppermute | solution.py:97
  11.8 3.7 %collective-permute-start.4 = (bf16[128,896]{1,0:T(8,128)(2,1)S(1)}, bf16[128,896]{1,0:T(8,128)(2,1)S(1)}, u32[]{:S(2)}, u32[]{:S(2)}) collective-permute-start(bf16[128,896]{1,0:T(8,128)(2,1)S(1)} %collective-permute-done.x_ref), channel_id=1, source_target_pairs={{0,1},{1,0},{2,3},{3,2},{4,5},{5,4},{6,7},{7,6},{8,9},{9,8},{10,11... | collective-permute-start | bytes 688136 | tf_op jit(solution)/shard_map/ppermute | solution.py:97
  15.5 1.9 %arrived_block.3 = bf16[128,896]{1,0:T(8,128)(2,1)S(1)} custom-call(bf16[128,896]{1,0:T(8,128)(2,1)S(1)} %collective-permute-done.x_ref, f32[1,896]{1,0:T(1,128)S(1)} %broadcast_in_dim.3.scale_ref, bf16[1216,896]{1,0:T(8,128)(2,1)S(1)} %get-tuple-element.14.gate_ref, bf16[1216,896]{1,0:T(8,128)(2,1)S(1)} %get-tuple-element.15.up_ref, ...), custom_call_target="tpu_custom_call" | custom-call | flops 836763648 | bytes 6537216 | tf_op jit(solution)/shard_map/arrived_block/pallas_call | solution.py:84
  17.4 2.5 %collective-permute-start.1 = (bf16[128,896]{1,0:T(8,128)(2,1)S(1)}, bf16[128,896]{1,0:T(8,128)(2,1)S(1)}, u32[]{:S(2)}, u32[]{:S(2)}) collective-permute-start(bf16[128,896]{1,0:T(8,128)(2,1)S(1)} %arrived_block.3), channel_id=1, source_target_pairs={{0,3},{1,2},{2,1},{3,0},{4,7},{5,6},{6,5},{7,4},{8,11},{9,10},{10,... | collective-permute-start | bytes 688136 | tf_op jit(solution)/shard_map/ppermute | solution.py:97
  20.0 0.0 collective-permute-done.2.x_ref
  20.0 1.9 %arrived_block.4 = bf16[128,896]{1,0:T(8,128)(2,1)S(1)} custom-call(bf16[128,896]{1,0:T(8,128)(2,1)S(1)} %collective-permute-done.2.x_ref, f32[1,896]{1,0:T(1,128)S(1)} %broadcast_in_dim.3.scale_ref, bf16[1216,896]{1,0:T(8,128)(2,1)S(1)} %get-tuple-element.14.gate_ref, bf16[1216,896]{1,0:T(8,128)(2,1)S(1)} %get-tuple-element.15.up_ref, ...), custom_call_target="tpu_custom_call" | custom-call | flops 836763648 | bytes 6537216 | tf_op jit(solution)/shard_map/arrived_block/pallas_call | solution.py:84
  21.9 0.1 collective-permute-start.3
  21.9 0.0 collective-permute-done.4.x_ref
  22.0 1.9 %arrived_block.5 = bf16[128,896]{1,0:T(8,128)(2,1)S(1)} custom-call(bf16[128,896]{1,0:T(8,128)(2,1)S(1)} %collective-permute-done.4.x_ref, f32[1,896]{1,0:T(1,128)S(1)} %broadcast_in_dim.3.scale_ref, bf16[1216,896]{1,0:T(8,128)(2,1)S(1)} %get-tuple-element.14.gate_ref, bf16[1216,896]{1,0:T(8,128)(2,1)S(1)} %get-tuple-element.15.up_ref, ...), custom_call_target="tpu_custom_call" | custom-call | flops 836763648 | bytes 6537216 | tf_op jit(solution)/shard_map/arrived_block/pallas_call | solution.py:84
  23.9 2.7 %collective-permute-start.5 = (bf16[128,896]{1,0:T(8,128)(2,1)S(1)}, bf16[128,896]{1,0:T(8,128)(2,1)S(1)}, u32[]{:S(2)}, u32[]{:S(2)}) collective-permute-start(bf16[128,896]{1,0:T(8,128)(2,1)S(1)} %arrived_block.5), channel_id=1, source_target_pairs={{0,2},{1,3},{2,0},{3,1},{4,6},{5,7},{6,4},{7,5},{8,10},{9,11},{10,... | collective-permute-start | bytes 688136 | tf_op jit(solution)/shard_map/ppermute | solution.py:97
  26.6 2.4 %collective-permute-done.1 = bf16[128,896]{1,0:T(8,128)(2,1)S(1)} collective-permute-done((bf16[128,896]{1,0:T(8,128)(2,1)S(1)}, bf16[128,896]{1,0:T(8,128)(2,1)S(1)}, u32[]{:S(2)}, u32[]{:S(2)}) %collective-permute-start.1) | collective-permute-done | bytes 229408 | tf_op jit(solution)/shard_map/ppermute | solution.py:97
  29.0 6.5 %collective-permute-done.3 = bf16[128,896]{1,0:T(8,128)(2,1)S(1)} collective-permute-done((bf16[128,896]{1,0:T(8,128)(2,1)S(1)}, bf16[128,896]{1,0:T(8,128)(2,1)S(1)}, u32[]{:S(2)}, u32[]{:S(2)}) %collective-permute-start.3) | collective-permute-done | bytes 229408 | tf_op jit(solution)/shard_map/ppermute | solution.py:97
  35.6 2.7 %collective-permute-done.5 = bf16[128,896]{1,0:T(8,128)(2,1)S(1)} collective-permute-done((bf16[128,896]{1,0:T(8,128)(2,1)S(1)}, bf16[128,896]{1,0:T(8,128)(2,1)S(1)}, u32[]{:S(2)}, u32[]{:S(2)}) %collective-permute-start.5) | collective-permute-done | bytes 229408 | tf_op jit(solution)/shard_map/ppermute | solution.py:97
  38.3 0.8 %add_convert_fusion = bf16[128,896]{1,0:T(8,128)(2,1)} fusion(bf16[128,896]{1,0:T(8,128)(2,1)S(1)} %collective-permute-done.5, bf16[128,896]{1,0:T(8,128)(2,1)S(1)} %collective-permute-done.3, f32[128,896]{1,0:T(8,128)S(1)} %get-tuple-element.12, bf16[128,896]{1,0:T(8,128)(2,1)S(1)} %collective-permute-done.1), kind=kLoop, calls=%fused_computation | loop fusion | flops 802816 | bytes 1376256 | tf_op jit(solution)/shard_map/convert_element_type | solution.py:112
Async XLA Ops:
  0.0 11.8 %collective-permute-start = (bf16[128,896]{1,0:T(8,128)(2,1)}, bf16[128,896]{1,0:T(8,128)(2,1)S(1)}, u32[]{:S(2)}, u32[]{:S(2)}) collective-permute-start(bf16[128,896]{1,0:T(8,128)(2,1)} %x_ref.1), channel_id=1, source_target_pairs={{0,3},{1,2},{2,1},{3,0},{4,7},{5,6},{6,5},{7,4},{8,11},{9,10},{10,... | collective-permute-start | bytes 688136 | tf_op jit(solution)/shard_map/ppermute | solution.py:97
  5.0 14.9 %collective-permute-start.2 = (bf16[128,896]{1,0:T(8,128)(2,1)}, bf16[128,896]{1,0:T(8,128)(2,1)S(1)}, u32[]{:S(2)}, u32[]{:S(2)}) collective-permute-start(bf16[128,896]{1,0:T(8,128)(2,1)} %x_ref.1), channel_id=1, source_target_pairs={{0,1},{1,0},{2,3},{3,2},{4,5},{5,4},{6,7},{7,6},{8,9},{9,8},{10,11... | collective-permute-start | bytes 688136 | tf_op jit(solution)/shard_map/ppermute | solution.py:97
  5.7 0.9 %copy-start = (bf16[128,896]{1,0:T(8,128)(2,1)S(1)}, bf16[128,896]{1,0:T(8,128)(2,1)}, u32[]{:S(2)}) copy-start(bf16[128,896]{1,0:T(8,128)(2,1)} %x_ref.1) | copy-start | bytes 688132
  11.8 10.2 %collective-permute-start.4 = (bf16[128,896]{1,0:T(8,128)(2,1)S(1)}, bf16[128,896]{1,0:T(8,128)(2,1)S(1)}, u32[]{:S(2)}, u32[]{:S(2)}) collective-permute-start(bf16[128,896]{1,0:T(8,128)(2,1)S(1)} %collective-permute-done.x_ref), channel_id=1, source_target_pairs={{0,1},{1,0},{2,3},{3,2},{4,5},{5,4},{6,7},{7,6},{8,9},{9,8},{10,11... | collective-permute-start | bytes 688136 | tf_op jit(solution)/shard_map/ppermute | solution.py:97
  17.4 11.6 %collective-permute-start.1 = (bf16[128,896]{1,0:T(8,128)(2,1)S(1)}, bf16[128,896]{1,0:T(8,128)(2,1)S(1)}, u32[]{:S(2)}, u32[]{:S(2)}) collective-permute-start(bf16[128,896]{1,0:T(8,128)(2,1)S(1)} %arrived_block.3), channel_id=1, source_target_pairs={{0,3},{1,2},{2,1},{3,0},{4,7},{5,6},{6,5},{7,4},{8,11},{9,10},{10,... | collective-permute-start | bytes 688136 | tf_op jit(solution)/shard_map/ppermute | solution.py:97
  21.9 13.7 %collective-permute-start.3 = (bf16[128,896]{1,0:T(8,128)(2,1)S(1)}, bf16[128,896]{1,0:T(8,128)(2,1)S(1)}, u32[]{:S(2)}, u32[]{:S(2)}) collective-permute-start(bf16[128,896]{1,0:T(8,128)(2,1)S(1)} %arrived_block.4), channel_id=1, source_target_pairs={{0,1},{1,0},{2,3},{3,2},{4,5},{5,4},{6,7},{7,6},{8,9},{9,8},{10,11... | collective-permute-start | bytes 688136 | tf_op jit(solution)/shard_map/ppermute | solution.py:97
  23.9 14.4 %collective-permute-start.5 = (bf16[128,896]{1,0:T(8,128)(2,1)S(1)}, bf16[128,896]{1,0:T(8,128)(2,1)S(1)}, u32[]{:S(2)}, u32[]{:S(2)}) collective-permute-start(bf16[128,896]{1,0:T(8,128)(2,1)S(1)} %arrived_block.5), channel_id=1, source_target_pairs={{0,2},{1,3},{2,0},{3,1},{4,6},{5,7},{6,4},{7,5},{8,10},{9,11},{10,... | collective-permute-start | bytes 688136 | tf_op jit(solution)/shard_map/ppermute | solution.py:97

commit v6 on v5

--- a/solution.py
+++ b/solution.py
@@ -106,9 +106,11 @@
     x_1 = hop(tokens, across[1])
     x_3, own = lax.optimization_barrier((hop(tokens, across[3]), own))
     x_2 = hop(x_3, across[1])
-    own = own.astype(jnp.float32)
-    for x, distance in ((x_3, 3), (x_1, 1), (x_2, 2)):
-        own = own + hop(arrived_block(x, scale, weights, jnp.bfloat16), across[distance]).astype(jnp.float32)
+    from_mirror = hop(arrived_block(x_3, scale, weights, jnp.bfloat16), across[3])
+    part_1 = arrived_block(x_1, scale, weights, jnp.bfloat16)
+    part_2, part_1 = lax.optimization_barrier((arrived_block(x_2, scale, weights, jnp.bfloat16), part_1))
+    for arrived in (from_mirror, hop(part_2, across[2]), hop(part_1, across[1])):
+        own = own + arrived.astype(jnp.float32)
     return own.astype(jnp.bfloat16)
 
 

time: 39.3 us -> 39.3 us (level)
  transfers between devices with their start and end apart: 6 -> 6, of which waited for: 4 -> 3; matrix products, arithmetic and copies ran while one was open for 2% -> 2% of each run, Pallas kernels for 25% -> 25%
where the time goes in v6:
time: 39.3 us; the launch traced here: 39.1 us
  starting transfers between devices  14.2 us (36%)
  waiting for transfers between devices  12.8 us (33%)
  Pallas kernels  9.75 us (25%)
  local copies, waits for them, and re-layouts  1.63 us (4%)
  other arithmetic  0.81 us (2%)
    ppermute x6, starting transfers between devices, hop(): return lax.ppermute(block, 'tensor', route)  14.2 us
    ppermute x6, waiting for transfers between devices, hop(): return lax.ppermute(block, 'tensor', route)  12.8 us
    pallas_call x3, Pallas kernels, arrived_block(): pl.pallas_call(arrived_kernel, out_shape=jax.ShapeDtypeStruct((rows, widt...  5.72 us
    pallas_call x1, Pallas kernels, own_block(): pl.pallas_call(own_kernel, out_shape=(jax.ShapeDtypeStruct((rows, width),...  4.03 us
    unnamed x2, local copies, waits for them, and re-layouts  0.94 us
    convert_element_type x1, other arithmetic, line_of_four(): return own.astype(jnp.bfloat16)  0.81 us
  transfers between devices with their start and end apart: 6, of which 3 were waited for; matrix products, arithmetic and copies ran while one was open for 2% of the time, Pallas kernels for 25%

profile of v6, /device:TPU:0, one launch (start us, length us, event | category | flops | bytes accessed | tf_op | source)
XLA Modules:
  0.0 39.1 jit_solution(9178573651484215444)
XLA Ops:
  0.0 5.0 %collective-permute-start = (bf16[128,896]{1,0:T(8,128)(2,1)}, bf16[128,896]{1,0:T(8,128)(2,1)S(1)}, u32[]{:S(2)}, u32[]{:S(2)}) collective-permute-start(bf16[128,896]{1,0:T(8,128)(2,1)} %x_ref.1), channel_id=1, source_target_pairs={{0,3},{1,2},{2,1},{3,0},{4,7},{5,6},{6,5},{7,4},{8,11},{9,10},{10,... | collective-permute-start | bytes 688136 | tf_op jit(solution)/shard_map/ppermute | solution.py:97
  5.0 0.0 collective-permute-start.3
  5.1 0.7 %broadcast_in_dim.3.scale_ref = f32[1,896]{1,0:T(1,128)S(1)} reshape(f32[896]{0:T(1024)} %param.6) | data formatting | bytes 7168 | tf_op jit(solution)/shard_map/broadcast_in_dim | solution.py:130
  5.7 0.0 copy-start
  5.7 0.9 %copy-done = bf16[128,896]{1,0:T(8,128)(2,1)S(1)} copy-done((bf16[128,896]{1,0:T(8,128)(2,1)S(1)}, bf16[128,896]{1,0:T(8,128)(2,1)}, u32[]{:S(2)}) %copy-start) | copy-done | bytes 229400
  6.7 4.0 %own_block.1 = (f32[128,896]{1,0:T(8,128)S(1)}, bf16[1216,896]{1,0:T(8,128)(2,1)S(1)}, bf16[1216,896]{1,0:T(8,128)(2,1)S(1)}, bf16[1216,896]{1,0:T(8,128)(2,1)S(1)}) custom-call(bf16[128,896]{1,0:T(8,128)(2,1)S(1)} %copy-done, f32[1,896]{1,0:T(1,128)S(1)} %broadcast_in_dim.3.scale_ref, bf16[1216,896]{1,0:T(8,128)(2,1)} %gate_hbm.1, ...), custom_call_target="tpu_custom_call" | custom-call | flops 836763648 | bytes 6537216 | tf_op jit(solution)/shard_map/own_block/pallas_call | solution.py:68
  10.7 1.1 %collective-permute-done.x_ref = bf16[128,896]{1,0:T(8,128)(2,1)S(1)} collective-permute-done((bf16[128,896]{1,0:T(8,128)(2,1)}, bf16[128,896]{1,0:T(8,128)(2,1)S(1)}, u32[]{:S(2)}, u32[]{:S(2)}) %collective-permute-start) | collective-permute-done | bytes 229408 | tf_op jit(solution)/shard_map/ppermute | solution.py:97
  11.8 3.7 %collective-permute-start.2 = (bf16[128,896]{1,0:T(8,128)(2,1)S(1)}, bf16[128,896]{1,0:T(8,128)(2,1)S(1)}, u32[]{:S(2)}, u32[]{:S(2)}) collective-permute-start(bf16[128,896]{1,0:T(8,128)(2,1)S(1)} %collective-permute-done.x_ref), channel_id=1, source_target_pairs={{0,1},{1,0},{2,3},{3,2},{4,5},{5,4},{6,7},{7,6},{8,9},{9,8},{10,11... | collective-permute-start | bytes 688136 | tf_op jit(solution)/shard_map/ppermute | solution.py:97
  15.5 1.9 %arrived_block.3 = bf16[128,896]{1,0:T(8,128)(2,1)S(1)} custom-call(bf16[128,896]{1,0:T(8,128)(2,1)S(1)} %collective-permute-done.x_ref, f32[1,896]{1,0:T(1,128)S(1)} %broadcast_in_dim.3.scale_ref, bf16[1216,896]{1,0:T(8,128)(2,1)S(1)} %get-tuple-element.16.gate_ref, bf16[1216,896]{1,0:T(8,128)(2,1)S(1)} %get-tuple-element.17.up_ref, ...), custom_call_target="tpu_custom_call" | custom-call | flops 836763648 | bytes 6537216 | tf_op jit(solution)/shard_map/arrived_block/pallas_call | solution.py:84
  17.4 2.5 %collective-permute-start.1 = (bf16[128,896]{1,0:T(8,128)(2,1)S(1)}, bf16[128,896]{1,0:T(8,128)(2,1)S(1)}, u32[]{:S(2)}, u32[]{:S(2)}) collective-permute-start(bf16[128,896]{1,0:T(8,128)(2,1)S(1)} %arrived_block.3), channel_id=1, source_target_pairs={{0,3},{1,2},{2,1},{3,0},{4,7},{5,6},{6,5},{7,4},{8,11},{9,10},{10,... | collective-permute-start | bytes 688136 | tf_op jit(solution)/shard_map/ppermute | solution.py:97
  20.0 0.0 collective-permute-done.3.x_ref
  20.0 1.9 %arrived_block.5 = bf16[128,896]{1,0:T(8,128)(2,1)S(1)} custom-call(bf16[128,896]{1,0:T(8,128)(2,1)S(1)} %collective-permute-done.3.x_ref, f32[1,896]{1,0:T(1,128)S(1)} %broadcast_in_dim.3.scale_ref, bf16[1216,896]{1,0:T(8,128)(2,1)S(1)} %get-tuple-element.16.gate_ref, bf16[1216,896]{1,0:T(8,128)(2,1)S(1)} %get-tuple-element.17.up_ref, ...), custom_call_target="tpu_custom_call" | custom-call | flops 836763648 | bytes 6537216 | tf_op jit(solution)/shard_map/arrived_block/pallas_call | solution.py:84
  21.9 0.0 collective-permute-done.2.x_ref
  21.9 1.9 %arrived_block.4 = bf16[128,896]{1,0:T(8,128)(2,1)S(1)} custom-call(bf16[128,896]{1,0:T(8,128)(2,1)S(1)} %collective-permute-done.2.x_ref, f32[1,896]{1,0:T(1,128)S(1)} %broadcast_in_dim.3.scale_ref, bf16[1216,896]{1,0:T(8,128)(2,1)S(1)} %get-tuple-element.16.gate_ref, bf16[1216,896]{1,0:T(8,128)(2,1)S(1)} %get-tuple-element.17.up_ref, ...), custom_call_target="tpu_custom_call" | custom-call | flops 836763648 | bytes 6537216 | tf_op jit(solution)/shard_map/arrived_block/pallas_call | solution.py:84
  23.8 2.8 %collective-permute-start.4 = (bf16[128,896]{1,0:T(8,128)(2,1)S(1)}, bf16[128,896]{1,0:T(8,128)(2,1)S(1)}, u32[]{:S(2)}, u32[]{:S(2)}) collective-permute-start(bf16[128,896]{1,0:T(8,128)(2,1)S(1)} %arrived_block.4), channel_id=1, source_target_pairs={{0,2},{1,3},{2,0},{3,1},{4,6},{5,7},{6,4},{7,5},{8,10},{9,11},{10,... | collective-permute-start | bytes 688136 | tf_op jit(solution)/shard_map/ppermute | solution.py:97
  26.6 0.0 collective-permute-start.5
  26.6 2.2 %collective-permute-done.1 = bf16[128,896]{1,0:T(8,128)(2,1)S(1)} collective-permute-done((bf16[128,896]{1,0:T(8,128)(2,1)S(1)}, bf16[128,896]{1,0:T(8,128)(2,1)S(1)}, u32[]{:S(2)}, u32[]{:S(2)}) %collective-permute-start.1) | collective-permute-done | bytes 229408 | tf_op jit(solution)/shard_map/ppermute | solution.py:97
  28.8 9.5 %collective-permute-done.4 = bf16[128,896]{1,0:T(8,128)(2,1)S(1)} collective-permute-done((bf16[128,896]{1,0:T(8,128)(2,1)S(1)}, bf16[128,896]{1,0:T(8,128)(2,1)S(1)}, u32[]{:S(2)}, u32[]{:S(2)}) %collective-permute-start.4) | collective-permute-done | bytes 229408 | tf_op jit(solution)/shard_map/ppermute | solution.py:97
  38.3 0.0 collective-permute-done.5
  38.3 0.8 %add_convert_fusion = bf16[128,896]{1,0:T(8,128)(2,1)} fusion(bf16[128,896]{1,0:T(8,128)(2,1)S(1)} %collective-permute-done.5, bf16[128,896]{1,0:T(8,128)(2,1)S(1)} %collective-permute-done.4, f32[128,896]{1,0:T(8,128)S(1)} %get-tuple-element.14, bf16[128,896]{1,0:T(8,128)(2,1)S(1)} %collective-permute-done.1), kind=kLoop, calls=%fused_computation | loop fusion | flops 802816 | bytes 1376256 | tf_op jit(solution)/shard_map/convert_element_type | solution.py:114
Async XLA Ops:
  0.0 11.8 %collective-permute-start = (bf16[128,896]{1,0:T(8,128)(2,1)}, bf16[128,896]{1,0:T(8,128)(2,1)S(1)}, u32[]{:S(2)}, u32[]{:S(2)}) collective-permute-start(bf16[128,896]{1,0:T(8,128)(2,1)} %x_ref.1), channel_id=1, source_target_pairs={{0,3},{1,2},{2,1},{3,0},{4,7},{5,6},{6,5},{7,4},{8,11},{9,10},{10,... | collective-permute-start | bytes 688136 | tf_op jit(solution)/shard_map/ppermute | solution.py:97
  5.0 14.9 %collective-permute-start.3 = (bf16[128,896]{1,0:T(8,128)(2,1)}, bf16[128,896]{1,0:T(8,128)(2,1)S(1)}, u32[]{:S(2)}, u32[]{:S(2)}) collective-permute-start(bf16[128,896]{1,0:T(8,128)(2,1)} %x_ref.1), channel_id=1, source_target_pairs={{0,1},{1,0},{2,3},{3,2},{4,5},{5,4},{6,7},{7,6},{8,9},{9,8},{10,11... | collective-permute-start | bytes 688136 | tf_op jit(solution)/shard_map/ppermute | solution.py:97
  5.7 0.9 %copy-start = (bf16[128,896]{1,0:T(8,128)(2,1)S(1)}, bf16[128,896]{1,0:T(8,128)(2,1)}, u32[]{:S(2)}) copy-start(bf16[128,896]{1,0:T(8,128)(2,1)} %x_ref.1) | copy-start | bytes 688132
  11.8 10.1 %collective-permute-start.2 = (bf16[128,896]{1,0:T(8,128)(2,1)S(1)}, bf16[128,896]{1,0:T(8,128)(2,1)S(1)}, u32[]{:S(2)}, u32[]{:S(2)}) collective-permute-start(bf16[128,896]{1,0:T(8,128)(2,1)S(1)} %collective-permute-done.x_ref), channel_id=1, source_target_pairs={{0,1},{1,0},{2,3},{3,2},{4,5},{5,4},{6,7},{7,6},{8,9},{9,8},{10,11... | collective-permute-start | bytes 688136 | tf_op jit(solution)/shard_map/ppermute | solution.py:97
  17.4 11.4 %collective-permute-start.1 = (bf16[128,896]{1,0:T(8,128)(2,1)S(1)}, bf16[128,896]{1,0:T(8,128)(2,1)S(1)}, u32[]{:S(2)}, u32[]{:S(2)}) collective-permute-start(bf16[128,896]{1,0:T(8,128)(2,1)S(1)} %arrived_block.3), channel_id=1, source_target_pairs={{0,3},{1,2},{2,1},{3,0},{4,7},{5,6},{6,5},{7,4},{8,11},{9,10},{10,... | collective-permute-start | bytes 688136 | tf_op jit(solution)/shard_map/ppermute | solution.py:97
  23.8 14.5 %collective-permute-start.4 = (bf16[128,896]{1,0:T(8,128)(2,1)S(1)}, bf16[128,896]{1,0:T(8,128)(2,1)S(1)}, u32[]{:S(2)}, u32[]{:S(2)}) collective-permute-start(bf16[128,896]{1,0:T(8,128)(2,1)S(1)} %arrived_block.4), channel_id=1, source_target_pairs={{0,2},{1,3},{2,0},{3,1},{4,6},{5,7},{6,4},{7,5},{8,10},{9,11},{10,... | collective-permute-start | bytes 688136 | tf_op jit(solution)/shard_map/ppermute | solution.py:97
  26.6 11.7 %collective-permute-start.5 = (bf16[128,896]{1,0:T(8,128)(2,1)S(1)}, bf16[128,896]{1,0:T(8,128)(2,1)S(1)}, u32[]{:S(2)}, u32[]{:S(2)}) collective-permute-start(bf16[128,896]{1,0:T(8,128)(2,1)S(1)} %arrived_block.5), channel_id=1, source_target_pairs={{0,1},{1,0},{2,3},{3,2},{4,5},{5,4},{6,7},{7,6},{8,9},{9,8},{10,11... | collective-permute-start | bytes 688136 | tf_op jit(solution)/shard_map/ppermute | solution.py:97

commit v7 on v4

--- a/solution.py
+++ b/solution.py
@@ -93,8 +93,8 @@
     )(x, scale, *weights)
 
 
-def hop(block, route):
-    return lax.ppermute(block, "tensor", route)
+def hop(block, route, axes="tensor"):
+    return lax.ppermute(block, axes, route)
 
 
 def add(arrived, part):
@@ -102,15 +102,22 @@
 
 
 def line_of_four(tokens, own, scale, weights):
-    across = {distance: [(place, place ^ distance) for place in range(4)] for distance in (1, 2, 3)}
-    x_1 = hop(tokens, across[1])
-    x_2, own = lax.optimization_barrier((hop(tokens, across[2]), own))
+    beside = [(place, place ^ 1) for place in range(4)]
+    groups = range(lax.axis_size("dp"))
+
+    def far(distances):
+        return [(group * 4 + place, group * 4 + (place ^ distances[group % 2])) for group in groups for place in range(4)]
+
+    def far_hop(block, distances):
+        return hop(block, far(distances), ("dp", "tensor"))
+
+    x_1 = hop(tokens, beside)
+    x_far, own = lax.optimization_barrier((far_hop(tokens, (2, 3)), own))
     part_1 = arrived_block(x_1, scale, weights, jnp.bfloat16)
-    x_3 = hop(x_2, across[1])
-    beside = hop(arrived_block(x_2, scale, weights, jnp.bfloat16), across[1])
-    from_neighbour = hop(part_1, across[1])
-    part_3 = arrived_block(x_3, scale, weights, jnp.float32)
-    from_far = hop(add(beside, part_3), across[3])
+    x_last = hop(x_far, beside)
+    joining = hop(arrived_block(x_far, scale, weights, jnp.bfloat16), beside)
+    from_neighbour = hop(part_1, beside)
+    from_far = far_hop(add(joining, arrived_block(x_last, scale, weights, jnp.float32)), (3, 2))
     return (own + from_neighbour.astype(jnp.float32) + from_far.astype(jnp.float32)).astype(jnp.bfloat16)
 
 

time: 39.9 us -> 38 us (0.952)
  waiting for transfers between devices: 15.4 us -> 12.6 us
  starting transfers between devices: 12.1 us -> 12.7 us
    ppermute x6, waiting for transfers between devices: 15.4 us -> 12.6 us  [hop(): return lax.ppermute(block, axes, route)]
    ppermute x6, starting transfers between devices: 12.1 us -> 12.7 us  [hop(): return lax.ppermute(block, axes, route)]
  transfers between devices with their start and end apart: 6 -> 6, of which waited for: 4 -> 5; matrix products, arithmetic and copies ran while one was open for 2% -> 2% of each run, Pallas kernels for 25% -> 26%
where the time goes in v7:
time: 38 us; the launch traced here: 37.5 us
  starting transfers between devices  12.7 us (33%)
  waiting for transfers between devices  12.6 us (33%)
  Pallas kernels  9.76 us (26%)
  local copies, waits for them, and re-layouts  1.63 us (4%)
  other arithmetic  0.8 us (2%)
    ppermute x6, starting transfers between devices, hop(): return lax.ppermute(block, axes, route)  12.7 us
    ppermute x6, waiting for transfers between devices, hop(): return lax.ppermute(block, axes, route)  12.6 us
    pallas_call x3, Pallas kernels, arrived_block(): pl.pallas_call(arrived_kernel, out_shape=jax.ShapeDtypeStruct((rows, widt...  5.72 us
    pallas_call x1, Pallas kernels, own_block(): pl.pallas_call(own_kernel, out_shape=(jax.ShapeDtypeStruct((rows, width),...  4.04 us
    unnamed x2, local copies, waits for them, and re-layouts  0.94 us
  transfers between devices with their start and end apart: 6, of which 5 were waited for; matrix products, arithmetic and copies ran while one was open for 2% of the time, Pallas kernels for 26%

profile of v7, /device:TPU:0, one launch (start us, length us, event | category | flops | bytes accessed | tf_op | source)
XLA Modules:
  0.0 37.5 jit_solution(10303526248724090794)
XLA Ops:
  0.0 4.0 %collective-permute-start = (bf16[128,896]{1,0:T(8,128)(2,1)}, bf16[128,896]{1,0:T(8,128)(2,1)S(1)}, u32[]{:S(2)}, u32[]{:S(2)}) collective-permute-start(bf16[128,896]{1,0:T(8,128)(2,1)} %x_ref.1), channel_id=1, source_target_pairs={{0,2},{1,3},{2,0},{3,1},{4,7},{5,6},{6,5},{7,4},{8,10},{9,11},{10,... | collective-permute-start | bytes 688136 | tf_op jit(solution)/shard_map/ppermute | solution.py:97
  4.0 1.6 %collective-permute-start.1 = (bf16[128,896]{1,0:T(8,128)(2,1)}, bf16[128,896]{1,0:T(8,128)(2,1)S(1)}, u32[]{:S(2)}, u32[]{:S(2)}) collective-permute-start(bf16[128,896]{1,0:T(8,128)(2,1)} %x_ref.1), channel_id=1, source_target_pairs={{0,1},{1,0},{2,3},{3,2},{4,5},{5,4},{6,7},{7,6},{8,9},{9,8},{10,11... | collective-permute-start | bytes 688136 | tf_op jit(solution)/shard_map/ppermute | solution.py:97
  5.6 0.7 %broadcast_in_dim.3.scale_ref = f32[1,896]{1,0:T(1,128)S(1)} reshape(f32[896]{0:T(1024)} %param.6) | data formatting | bytes 7168 | tf_op jit(solution)/shard_map/broadcast_in_dim | solution.py:137
  6.3 0.0 copy-start
  6.3 0.9 %copy-done = bf16[128,896]{1,0:T(8,128)(2,1)S(1)} copy-done((bf16[128,896]{1,0:T(8,128)(2,1)S(1)}, bf16[128,896]{1,0:T(8,128)(2,1)}, u32[]{:S(2)}) %copy-start) | copy-done | bytes 229400
  7.2 4.0 %own_block.1 = (f32[128,896]{1,0:T(8,128)S(1)}, bf16[1216,896]{1,0:T(8,128)(2,1)S(1)}, bf16[1216,896]{1,0:T(8,128)(2,1)S(1)}, bf16[1216,896]{1,0:T(8,128)(2,1)S(1)}) custom-call(bf16[128,896]{1,0:T(8,128)(2,1)S(1)} %copy-done, f32[1,896]{1,0:T(1,128)S(1)} %broadcast_in_dim.3.scale_ref, bf16[1216,896]{1,0:T(8,128)(2,1)} %gate_hbm.1, ...), custom_call_target="tpu_custom_call" | custom-call | flops 836763648 | bytes 6537216 | tf_op jit(solution)/shard_map/own_block/pallas_call | solution.py:68
  11.3 3.7 %collective-permute-done.x_ref = bf16[128,896]{1,0:T(8,128)(2,1)S(1)} collective-permute-done((bf16[128,896]{1,0:T(8,128)(2,1)}, bf16[128,896]{1,0:T(8,128)(2,1)S(1)}, u32[]{:S(2)}, u32[]{:S(2)}) %collective-permute-start) | collective-permute-done | bytes 229408 | tf_op jit(solution)/shard_map/ppermute | solution.py:97
  15.0 0.0 collective-permute-start.4
  15.0 1.9 %arrived_block.4 = bf16[128,896]{1,0:T(8,128)(2,1)S(1)} custom-call(bf16[128,896]{1,0:T(8,128)(2,1)S(1)} %collective-permute-done.x_ref, f32[1,896]{1,0:T(1,128)S(1)} %broadcast_in_dim.3.scale_ref, bf16[1216,896]{1,0:T(8,128)(2,1)S(1)} %get-tuple-element.13.gate_ref, bf16[1216,896]{1,0:T(8,128)(2,1)S(1)} %get-tuple-element.14.up_ref, ...), custom_call_target="tpu_custom_call" | custom-call | flops 836763648 | bytes 6537216 | tf_op jit(solution)/shard_map/arrived_block/pallas_call | solution.py:84
  17.0 2.1 %collective-permute-start.3 = (bf16[128,896]{1,0:T(8,128)(2,1)S(1)}, bf16[128,896]{1,0:T(8,128)(2,1)S(1)}, u32[]{:S(2)}, u32[]{:S(2)}) collective-permute-start(bf16[128,896]{1,0:T(8,128)(2,1)S(1)} %arrived_block.4), channel_id=1, source_target_pairs={{0,1},{1,0},{2,3},{3,2},{4,5},{5,4},{6,7},{7,6},{8,9},{9,8},{10,11... | collective-permute-start | bytes 688136 | tf_op jit(solution)/shard_map/ppermute | solution.py:97
  19.1 0.0 collective-permute-done.1.x_ref
  19.1 1.9 %arrived_block.3 = bf16[128,896]{1,0:T(8,128)(2,1)S(1)} custom-call(bf16[128,896]{1,0:T(8,128)(2,1)S(1)} %collective-permute-done.1.x_ref, f32[1,896]{1,0:T(1,128)S(1)} %broadcast_in_dim.3.scale_ref, bf16[1216,896]{1,0:T(8,128)(2,1)S(1)} %get-tuple-element.13.gate_ref, bf16[1216,896]{1,0:T(8,128)(2,1)S(1)} %get-tuple-element.14.up_ref, ...), custom_call_target="tpu_custom_call" | custom-call | flops 836763648 | bytes 6537216 | tf_op jit(solution)/shard_map/arrived_block/pallas_call | solution.py:84
  21.0 0.1 collective-permute-start.2
  21.1 1.8 %collective-permute-done.4.x_ref = bf16[128,896]{1,0:T(8,128)(2,1)S(1)} collective-permute-done((bf16[128,896]{1,0:T(8,128)(2,1)S(1)}, bf16[128,896]{1,0:T(8,128)(2,1)S(1)}, u32[]{:S(2)}, u32[]{:S(2)}) %collective-permute-start.4) | collective-permute-done | bytes 229408 | tf_op jit(solution)/shard_map/ppermute | solution.py:97
  22.9 1.9 %arrived_block.5 = f32[128,896]{1,0:T(8,128)S(1)} custom-call(bf16[128,896]{1,0:T(8,128)(2,1)S(1)} %collective-permute-done.4.x_ref, f32[1,896]{1,0:T(1,128)S(1)} %broadcast_in_dim.3.scale_ref, bf16[1216,896]{1,0:T(8,128)(2,1)S(1)} %get-tuple-element.13.gate_ref, bf16[1216,896]{1,0:T(8,128)(2,1)S(1)} %get-tuple-element.14.up_ref, ...), custom_call_target="tpu_custom_call" | custom-call | flops 836763648 | bytes 6537216 | tf_op jit(solution)/shard_map/arrived_block/pallas_call | solution.py:84
  24.8 3.0 %collective-permute-done.3 = bf16[128,896]{1,0:T(8,128)(2,1)S(1)} collective-permute-done((bf16[128,896]{1,0:T(8,128)(2,1)S(1)}, bf16[128,896]{1,0:T(8,128)(2,1)S(1)}, u32[]{:S(2)}, u32[]{:S(2)}) %collective-permute-start.3) | collective-permute-done | bytes 229408 | tf_op jit(solution)/shard_map/ppermute | solution.py:97
  27.9 4.8 %collective-permute-start.5 = (bf16[128,896]{1,0:T(8,128)(2,1)S(1)}, bf16[128,896]{1,0:T(8,128)(2,1)S(1)}, u32[]{:S(2)}, u32[]{:S(2)}) collective-permute-start(bf16[128,896]{1,0:T(8,128)(2,1)S(1)} %add_convert_fusion.1), channel_id=1, source_target_pairs={{0,3},{1,2},{2,1},{3,0},{4,6},{5,7},{6,4},{7,5},{8,11},{9,10},{10,... | collective-permute-start | bytes 688136 | tf_op jit(solution)/shard_map/ppermute | solution.py:97
  32.7 0.6 %collective-permute-done.2 = bf16[128,896]{1,0:T(8,128)(2,1)S(1)} collective-permute-done((bf16[128,896]{1,0:T(8,128)(2,1)S(1)}, bf16[128,896]{1,0:T(8,128)(2,1)S(1)}, u32[]{:S(2)}, u32[]{:S(2)}) %collective-permute-start.2) | collective-permute-done | bytes 229408 | tf_op jit(solution)/shard_map/ppermute | solution.py:97
  33.3 3.4 %collective-permute-done.5 = bf16[128,896]{1,0:T(8,128)(2,1)S(1)} collective-permute-done((bf16[128,896]{1,0:T(8,128)(2,1)S(1)}, bf16[128,896]{1,0:T(8,128)(2,1)S(1)}, u32[]{:S(2)}, u32[]{:S(2)}) %collective-permute-start.5) | collective-permute-done | bytes 229408 | tf_op jit(solution)/shard_map/ppermute | solution.py:97
  36.8 0.8 %add_convert_fusion = bf16[128,896]{1,0:T(8,128)(2,1)} fusion(bf16[128,896]{1,0:T(8,128)(2,1)S(1)} %collective-permute-done.5, f32[128,896]{1,0:T(8,128)S(1)} %get-tuple-element.12, bf16[128,896]{1,0:T(8,128)(2,1)S(1)} %collective-permute-done.2), kind=kLoop, calls=%fused_computation | loop fusion | flops 573440 | bytes 1146880 | tf_op jit(solution)/shard_map/convert_element_type | solution.py:121
  (1 shorter events, 0.0 us)
Async XLA Ops:
  0.0 15.0 %collective-permute-start = (bf16[128,896]{1,0:T(8,128)(2,1)}, bf16[128,896]{1,0:T(8,128)(2,1)S(1)}, u32[]{:S(2)}, u32[]{:S(2)}) collective-permute-start(bf16[128,896]{1,0:T(8,128)(2,1)} %x_ref.1), channel_id=1, source_target_pairs={{0,2},{1,3},{2,0},{3,1},{4,7},{5,6},{6,5},{7,4},{8,10},{9,11},{10,... | collective-permute-start | bytes 688136 | tf_op jit(solution)/shard_map/ppermute | solution.py:97
  4.0 15.0 %collective-permute-start.1 = (bf16[128,896]{1,0:T(8,128)(2,1)}, bf16[128,896]{1,0:T(8,128)(2,1)S(1)}, u32[]{:S(2)}, u32[]{:S(2)}) collective-permute-start(bf16[128,896]{1,0:T(8,128)(2,1)} %x_ref.1), channel_id=1, source_target_pairs={{0,1},{1,0},{2,3},{3,2},{4,5},{5,4},{6,7},{7,6},{8,9},{9,8},{10,11... | collective-permute-start | bytes 688136 | tf_op jit(solution)/shard_map/ppermute | solution.py:97
  6.3 0.9 %copy-start = (bf16[128,896]{1,0:T(8,128)(2,1)S(1)}, bf16[128,896]{1,0:T(8,128)(2,1)}, u32[]{:S(2)}) copy-start(bf16[128,896]{1,0:T(8,128)(2,1)} %x_ref.1) | copy-start | bytes 688132
  15.0 7.9 %collective-permute-start.4 = (bf16[128,896]{1,0:T(8,128)(2,1)S(1)}, bf16[128,896]{1,0:T(8,128)(2,1)S(1)}, u32[]{:S(2)}, u32[]{:S(2)}) collective-permute-start(bf16[128,896]{1,0:T(8,128)(2,1)S(1)} %collective-permute-done.x_ref), channel_id=1, source_target_pairs={{0,1},{1,0},{2,3},{3,2},{4,5},{5,4},{6,7},{7,6},{8,9},{9,8},{10,11... | collective-permute-start | bytes 688136 | tf_op jit(solution)/shard_map/ppermute | solution.py:97
  17.0 10.9 %collective-permute-start.3 = (bf16[128,896]{1,0:T(8,128)(2,1)S(1)}, bf16[128,896]{1,0:T(8,128)(2,1)S(1)}, u32[]{:S(2)}, u32[]{:S(2)}) collective-permute-start(bf16[128,896]{1,0:T(8,128)(2,1)S(1)} %arrived_block.4), channel_id=1, source_target_pairs={{0,1},{1,0},{2,3},{3,2},{4,5},{5,4},{6,7},{7,6},{8,9},{9,8},{10,11... | collective-permute-start | bytes 688136 | tf_op jit(solution)/shard_map/ppermute | solution.py:97
  21.0 12.4 %collective-permute-start.2 = (bf16[128,896]{1,0:T(8,128)(2,1)S(1)}, bf16[128,896]{1,0:T(8,128)(2,1)S(1)}, u32[]{:S(2)}, u32[]{:S(2)}) collective-permute-start(bf16[128,896]{1,0:T(8,128)(2,1)S(1)} %arrived_block.3), channel_id=1, source_target_pairs={{0,1},{1,0},{2,3},{3,2},{4,5},{5,4},{6,7},{7,6},{8,9},{9,8},{10,11... | collective-permute-start | bytes 688136 | tf_op jit(solution)/shard_map/ppermute | solution.py:97
  27.9 8.9 %collective-permute-start.5 = (bf16[128,896]{1,0:T(8,128)(2,1)S(1)}, bf16[128,896]{1,0:T(8,128)(2,1)S(1)}, u32[]{:S(2)}, u32[]{:S(2)}) collective-permute-start(bf16[128,896]{1,0:T(8,128)(2,1)S(1)} %add_convert_fusion.1), channel_id=1, source_target_pairs={{0,3},{1,2},{2,1},{3,0},{4,6},{5,7},{6,4},{7,5},{8,11},{9,10},{10,... | collective-permute-start | bytes 688136 | tf_op jit(solution)/shard_map/ppermute | solution.py:97

commit v8 on v7

--- a/solution.py
+++ b/solution.py
@@ -116,8 +116,9 @@
     part_1 = arrived_block(x_1, scale, weights, jnp.bfloat16)
     x_last = hop(x_far, beside)
     joining = hop(arrived_block(x_far, scale, weights, jnp.bfloat16), beside)
+    part_last, part_1 = lax.optimization_barrier((arrived_block(x_last, scale, weights, jnp.float32), part_1))
     from_neighbour = hop(part_1, beside)
-    from_far = far_hop(add(joining, arrived_block(x_last, scale, weights, jnp.float32)), (3, 2))
+    from_far = far_hop(add(joining, part_last), (3, 2))
     return (own + from_neighbour.astype(jnp.float32) + from_far.astype(jnp.float32)).astype(jnp.bfloat16)
 
 

time: 38 us -> 38.3 us (level)
  waiting for transfers between devices: 12.6 us -> 16.4 us
  starting transfers between devices: 12.7 us -> 9.48 us
    ppermute x6, waiting for transfers between devices: 12.6 us -> 16.4 us  [hop(): return lax.ppermute(block, axes, route)]
    ppermute x6, starting transfers between devices: 12.7 us -> 9.48 us  [hop(): return lax.ppermute(block, axes, route)]
where the time goes in v8:
time: 38.3 us; the launch traced here: 38.1 us
  waiting for transfers between devices  16.4 us (43%)
  Pallas kernels  9.76 us (25%)
  starting transfers between devices  9.48 us (25%)
  local copies, waits for them, and re-layouts  1.63 us (4%)
  other arithmetic  0.8 us (2%)
    ppermute x6, waiting for transfers between devices, hop(): return lax.ppermute(block, axes, route)  16.4 us
    ppermute x6, starting transfers between devices, hop(): return lax.ppermute(block, axes, route)  9.48 us
    pallas_call x3, Pallas kernels, arrived_block(): pl.pallas_call(arrived_kernel, out_shape=jax.ShapeDtypeStruct((rows, widt...  5.72 us
    pallas_call x1, Pallas kernels, own_block(): pl.pallas_call(own_kernel, out_shape=(jax.ShapeDtypeStruct((rows, width),...  4.04 us
    unnamed x2, local copies, waits for them, and re-layouts  0.94 us
  transfers between devices with their start and end apart: 6, of which 5 were waited for; matrix products, arithmetic and copies ran while one was open for 2% of the time, Pallas kernels for 26%

profile of v8, /device:TPU:0, one launch (start us, length us, event | category | flops | bytes accessed | tf_op | source)
XLA Modules:
  0.0 38.1 jit_solution(17327789656106264390)
XLA Ops:
  0.0 4.0 %collective-permute-start = (bf16[128,896]{1,0:T(8,128)(2,1)}, bf16[128,896]{1,0:T(8,128)(2,1)S(1)}, u32[]{:S(2)}, u32[]{:S(2)}) collective-permute-start(bf16[128,896]{1,0:T(8,128)(2,1)} %x_ref.1), channel_id=1, source_target_pairs={{0,2},{1,3},{2,0},{3,1},{4,7},{5,6},{6,5},{7,4},{8,10},{9,11},{10,... | collective-permute-start | bytes 688136 | tf_op jit(solution)/shard_map/ppermute | solution.py:97
  4.0 1.6 %collective-permute-start.2 = (bf16[128,896]{1,0:T(8,128)(2,1)}, bf16[128,896]{1,0:T(8,128)(2,1)S(1)}, u32[]{:S(2)}, u32[]{:S(2)}) collective-permute-start(bf16[128,896]{1,0:T(8,128)(2,1)} %x_ref.1), channel_id=1, source_target_pairs={{0,1},{1,0},{2,3},{3,2},{4,5},{5,4},{6,7},{7,6},{8,9},{9,8},{10,11... | collective-permute-start | bytes 688136 | tf_op jit(solution)/shard_map/ppermute | solution.py:97
  5.6 0.7 %broadcast_in_dim.3.scale_ref = f32[1,896]{1,0:T(1,128)S(1)} reshape(f32[896]{0:T(1024)} %param.6) | data formatting | bytes 7168 | tf_op jit(solution)/shard_map/broadcast_in_dim | solution.py:138
  6.3 0.0 copy-start
  6.3 0.9 %copy-done = bf16[128,896]{1,0:T(8,128)(2,1)S(1)} copy-done((bf16[128,896]{1,0:T(8,128)(2,1)S(1)}, bf16[128,896]{1,0:T(8,128)(2,1)}, u32[]{:S(2)}) %copy-start) | copy-done | bytes 229400
  7.2 4.0 %own_block.1 = (f32[128,896]{1,0:T(8,128)S(1)}, bf16[1216,896]{1,0:T(8,128)(2,1)S(1)}, bf16[1216,896]{1,0:T(8,128)(2,1)S(1)}, bf16[1216,896]{1,0:T(8,128)(2,1)S(1)}) custom-call(bf16[128,896]{1,0:T(8,128)(2,1)S(1)} %copy-done, f32[1,896]{1,0:T(1,128)S(1)} %broadcast_in_dim.3.scale_ref, bf16[1216,896]{1,0:T(8,128)(2,1)} %gate_hbm.1, ...), custom_call_target="tpu_custom_call" | custom-call | flops 836763648 | bytes 6537216 | tf_op jit(solution)/shard_map/own_block/pallas_call | solution.py:68
  11.3 3.7 %collective-permute-done.x_ref = bf16[128,896]{1,0:T(8,128)(2,1)S(1)} collective-permute-done((bf16[128,896]{1,0:T(8,128)(2,1)}, bf16[128,896]{1,0:T(8,128)(2,1)S(1)}, u32[]{:S(2)}, u32[]{:S(2)}) %collective-permute-start) | collective-permute-done | bytes 229408 | tf_op jit(solution)/shard_map/ppermute | solution.py:97
  15.0 0.0 collective-permute-start.1
  15.0 1.9 %arrived_block.5 = bf16[128,896]{1,0:T(8,128)(2,1)S(1)} custom-call(bf16[128,896]{1,0:T(8,128)(2,1)S(1)} %collective-permute-done.x_ref, f32[1,896]{1,0:T(1,128)S(1)} %broadcast_in_dim.3.scale_ref, bf16[1216,896]{1,0:T(8,128)(2,1)S(1)} %get-tuple-element.16.gate_ref, bf16[1216,896]{1,0:T(8,128)(2,1)S(1)} %get-tuple-element.17.up_ref, ...), custom_call_target="tpu_custom_call" | custom-call | flops 836763648 | bytes 6537216 | tf_op jit(solution)/shard_map/arrived_block/pallas_call | solution.py:84
  17.0 2.1 %collective-permute-start.4 = (bf16[128,896]{1,0:T(8,128)(2,1)S(1)}, bf16[128,896]{1,0:T(8,128)(2,1)S(1)}, u32[]{:S(2)}, u32[]{:S(2)}) collective-permute-start(bf16[128,896]{1,0:T(8,128)(2,1)S(1)} %arrived_block.5), channel_id=1, source_target_pairs={{0,1},{1,0},{2,3},{3,2},{4,5},{5,4},{6,7},{7,6},{8,9},{9,8},{10,11... | collective-permute-start | bytes 688136 | tf_op jit(solution)/shard_map/ppermute | solution.py:97
  19.1 0.0 collective-permute-done.2.x_ref
  19.1 1.9 %arrived_block.4 = bf16[128,896]{1,0:T(8,128)(2,1)S(1)} custom-call(bf16[128,896]{1,0:T(8,128)(2,1)S(1)} %collective-permute-done.2.x_ref, f32[1,896]{1,0:T(1,128)S(1)} %broadcast_in_dim.3.scale_ref, bf16[1216,896]{1,0:T(8,128)(2,1)S(1)} %get-tuple-element.16.gate_ref, bf16[1216,896]{1,0:T(8,128)(2,1)S(1)} %get-tuple-element.17.up_ref, ...), custom_call_target="tpu_custom_call" | custom-call | flops 836763648 | bytes 6537216 | tf_op jit(solution)/shard_map/arrived_block/pallas_call | solution.py:84
  21.0 1.9 %collective-permute-done.1.x_ref = bf16[128,896]{1,0:T(8,128)(2,1)S(1)} collective-permute-done((bf16[128,896]{1,0:T(8,128)(2,1)S(1)}, bf16[128,896]{1,0:T(8,128)(2,1)S(1)}, u32[]{:S(2)}, u32[]{:S(2)}) %collective-permute-start.1) | collective-permute-done | bytes 229408 | tf_op jit(solution)/shard_map/ppermute | solution.py:97
  22.9 1.9 %arrived_block.3 = f32[128,896]{1,0:T(8,128)S(1)} custom-call(bf16[128,896]{1,0:T(8,128)(2,1)S(1)} %collective-permute-done.1.x_ref, f32[1,896]{1,0:T(1,128)S(1)} %broadcast_in_dim.3.scale_ref, bf16[1216,896]{1,0:T(8,128)(2,1)S(1)} %get-tuple-element.16.gate_ref, bf16[1216,896]{1,0:T(8,128)(2,1)S(1)} %get-tuple-element.17.up_ref, ...), custom_call_target="tpu_custom_call" | custom-call | flops 836763648 | bytes 6537216 | tf_op jit(solution)/shard_map/arrived_block/pallas_call | solution.py:84
  24.8 1.2 %collective-permute-done.4 = bf16[128,896]{1,0:T(8,128)(2,1)S(1)} collective-permute-done((bf16[128,896]{1,0:T(8,128)(2,1)S(1)}, bf16[128,896]{1,0:T(8,128)(2,1)S(1)}, u32[]{:S(2)}, u32[]{:S(2)}) %collective-permute-start.4) | collective-permute-done | bytes 229408 | tf_op jit(solution)/shard_map/ppermute | solution.py:97
  26.0 1.8 %collective-permute-start.5 = (bf16[128,896]{1,0:T(8,128)(2,1)S(1)}, bf16[128,896]{1,0:T(8,128)(2,1)S(1)}, u32[]{:S(2)}, u32[]{:S(2)}) collective-permute-start(bf16[128,896]{1,0:T(8,128)(2,1)S(1)} %add_convert_fusion.1), channel_id=1, source_target_pairs={{0,3},{1,2},{2,1},{3,0},{4,6},{5,7},{6,4},{7,5},{8,11},{9,10},{10,... | collective-permute-start | bytes 688136 | tf_op jit(solution)/shard_map/ppermute | solution.py:97
  27.8 0.0 collective-permute-start.3
  27.8 8.6 %collective-permute-done.5 = bf16[128,896]{1,0:T(8,128)(2,1)S(1)} collective-permute-done((bf16[128,896]{1,0:T(8,128)(2,1)S(1)}, bf16[128,896]{1,0:T(8,128)(2,1)S(1)}, u32[]{:S(2)}, u32[]{:S(2)}) %collective-permute-start.5) | collective-permute-done | bytes 229408 | tf_op jit(solution)/shard_map/ppermute | solution.py:97
  36.4 0.9 %collective-permute-done.3 = bf16[128,896]{1,0:T(8,128)(2,1)S(1)} collective-permute-done((bf16[128,896]{1,0:T(8,128)(2,1)S(1)}, bf16[128,896]{1,0:T(8,128)(2,1)S(1)}, u32[]{:S(2)}, u32[]{:S(2)}) %collective-permute-start.3) | collective-permute-done | bytes 229408 | tf_op jit(solution)/shard_map/ppermute | solution.py:97
  37.3 0.8 %add_convert_fusion = bf16[128,896]{1,0:T(8,128)(2,1)} fusion(bf16[128,896]{1,0:T(8,128)(2,1)S(1)} %collective-permute-done.5, f32[128,896]{1,0:T(8,128)S(1)} %get-tuple-element.14, bf16[128,896]{1,0:T(8,128)(2,1)S(1)} %collective-permute-done.3), kind=kLoop, calls=%fused_computation | loop fusion | flops 573440 | bytes 1146880 | tf_op jit(solution)/shard_map/convert_element_type | solution.py:122
  (1 shorter events, 0.0 us)
Async XLA Ops:
  0.0 15.0 %collective-permute-start = (bf16[128,896]{1,0:T(8,128)(2,1)}, bf16[128,896]{1,0:T(8,128)(2,1)S(1)}, u32[]{:S(2)}, u32[]{:S(2)}) collective-permute-start(bf16[128,896]{1,0:T(8,128)(2,1)} %x_ref.1), channel_id=1, source_target_pairs={{0,2},{1,3},{2,0},{3,1},{4,7},{5,6},{6,5},{7,4},{8,10},{9,11},{10,... | collective-permute-start | bytes 688136 | tf_op jit(solution)/shard_map/ppermute | solution.py:97
  4.0 15.0 %collective-permute-start.2 = (bf16[128,896]{1,0:T(8,128)(2,1)}, bf16[128,896]{1,0:T(8,128)(2,1)S(1)}, u32[]{:S(2)}, u32[]{:S(2)}) collective-permute-start(bf16[128,896]{1,0:T(8,128)(2,1)} %x_ref.1), channel_id=1, source_target_pairs={{0,1},{1,0},{2,3},{3,2},{4,5},{5,4},{6,7},{7,6},{8,9},{9,8},{10,11... | collective-permute-start | bytes 688136 | tf_op jit(solution)/shard_map/ppermute | solution.py:97
  6.3 0.9 %copy-start = (bf16[128,896]{1,0:T(8,128)(2,1)S(1)}, bf16[128,896]{1,0:T(8,128)(2,1)}, u32[]{:S(2)}) copy-start(bf16[128,896]{1,0:T(8,128)(2,1)} %x_ref.1) | copy-start | bytes 688132
  15.0 7.9 %collective-permute-start.1 = (bf16[128,896]{1,0:T(8,128)(2,1)S(1)}, bf16[128,896]{1,0:T(8,128)(2,1)S(1)}, u32[]{:S(2)}, u32[]{:S(2)}) collective-permute-start(bf16[128,896]{1,0:T(8,128)(2,1)S(1)} %collective-permute-done.x_ref), channel_id=1, source_target_pairs={{0,1},{1,0},{2,3},{3,2},{4,5},{5,4},{6,7},{7,6},{8,9},{9,8},{10,11... | collective-permute-start | bytes 688136 | tf_op jit(solution)/shard_map/ppermute | solution.py:97
  17.0 9.0 %collective-permute-start.4 = (bf16[128,896]{1,0:T(8,128)(2,1)S(1)}, bf16[128,896]{1,0:T(8,128)(2,1)S(1)}, u32[]{:S(2)}, u32[]{:S(2)}) collective-permute-start(bf16[128,896]{1,0:T(8,128)(2,1)S(1)} %arrived_block.5), channel_id=1, source_target_pairs={{0,1},{1,0},{2,3},{3,2},{4,5},{5,4},{6,7},{7,6},{8,9},{9,8},{10,11... | collective-permute-start | bytes 688136 | tf_op jit(solution)/shard_map/ppermute | solution.py:97
  26.0 10.4 %collective-permute-start.5 = (bf16[128,896]{1,0:T(8,128)(2,1)S(1)}, bf16[128,896]{1,0:T(8,128)(2,1)S(1)}, u32[]{:S(2)}, u32[]{:S(2)}) collective-permute-start(bf16[128,896]{1,0:T(8,128)(2,1)S(1)} %add_convert_fusion.1), channel_id=1, source_target_pairs={{0,3},{1,2},{2,1},{3,0},{4,6},{5,7},{6,4},{7,5},{8,11},{9,10},{10,... | collective-permute-start | bytes 688136 | tf_op jit(solution)/shard_map/ppermute | solution.py:97
  27.8 9.6 %collective-permute-start.3 = (bf16[128,896]{1,0:T(8,128)(2,1)S(1)}, bf16[128,896]{1,0:T(8,128)(2,1)S(1)}, u32[]{:S(2)}, u32[]{:S(2)}) collective-permute-start(bf16[128,896]{1,0:T(8,128)(2,1)S(1)} %arrived_block.4), channel_id=1, source_target_pairs={{0,1},{1,0},{2,3},{3,2},{4,5},{5,4},{6,7},{7,6},{8,9},{9,8},{10,11... | collective-permute-start | bytes 688136 | tf_op jit(solution)/shard_map/ppermute | solution.py:97

commit v9 on v7

--- a/solution.py
+++ b/solution.py
@@ -27,7 +27,11 @@
     return (x.astype(jnp.float32) / scale).astype(jnp.bfloat16)
 
 
-def own_kernel(x_ref, scale_ref, gate_hbm, up_hbm, down_hbm, out_ref, gate_ref, up_ref, down_ref, hidden, sems):
+def second_core():
+    return lax.rem(lax.axis_index("dp"), 2) == 1
+
+
+def own_kernel(x_ref, scale_ref, gate_hbm, up_hbm, down_hbm, out_ref, held_ref, gate_ref, up_ref, down_ref, hidden, sems):
     tiles = unit_tiles(gate_hbm.shape[0])
     copies = [
         [
@@ -41,22 +45,48 @@
         for copy in pair:
             copy.start()
     down_copy.start()
+    held_ref[...] = x_ref[...]
     x = smooth(x_ref[...], scale_ref[...])
     for pair, tile in zip(copies, tiles):
         for copy in pair:
             copy.wait()
-        hidden[:, tile] = hidden_tile(x, gate_ref[tile, :], up_ref[tile, :])
+
+        @pl.when(jnp.logical_not(second_core()))
+        def _():
+            hidden[:, tile] = hidden_tile(x, gate_ref[tile, :], up_ref[tile, :])
+
     down_copy.wait()
-    out_ref[...] = jnp.dot(hidden[...], down_ref[...], preferred_element_type=jnp.float32)
-
-
-def arrived_kernel(x_ref, scale_ref, gate_ref, up_ref, down_ref, out_ref, hidden):
+
+    @pl.when(jnp.logical_not(second_core()))
+    def _():
+        out_ref[...] = jnp.dot(hidden[...], down_ref[...], preferred_element_type=jnp.float32)
+
+
+def multiply(x_ref, scale_ref, gate_ref, up_ref, down_ref, out_ref, hidden):
     x = smooth(x_ref[...], scale_ref[...])
     for tile in unit_tiles(gate_ref.shape[0]):
         hidden[:, tile] = hidden_tile(x, gate_ref[tile, :], up_ref[tile, :])
     out_ref[...] = jnp.dot(hidden[...], down_ref[...], preferred_element_type=jnp.float32).astype(out_ref.dtype)
 
 
+def arrived_kernel(x_ref, *refs):
+    multiply(x_ref, *refs)
+
+
+def arrived_and_own_kernel(x_ref, scale_ref, gate_ref, up_ref, down_ref, held_ref, own_ref, out_ref, own_out, hidden):
+    weights = (scale_ref, gate_ref, up_ref, down_ref)
+
+    @pl.when(second_core())
+    def _():
+        multiply(held_ref, *weights, own_out, hidden)
+
+    @pl.when(jnp.logical_not(second_core()))
+    def _():
+        own_out[...] = own_ref[...]
+
+    multiply(x_ref, *weights, out_ref, hidden)
+
+
 def cost(rows, width, units):
     return pl.CostEstimate(flops=6 * rows * width * units, bytes_accessed=6 * units * width, transcendentals=2 * rows * units)
 
@@ -65,17 +95,17 @@
     rows, width = x.shape
     units = weights[0].shape[0]
     held = tuple(jax.ShapeDtypeStruct(w.shape, w.dtype) for w in weights)
-    part, *kept = pl.pallas_call(
+    part, tokens, *kept = pl.pallas_call(
         own_kernel,
-        out_shape=(jax.ShapeDtypeStruct((rows, width), jnp.float32),) + held,
+        out_shape=(jax.ShapeDtypeStruct((rows, width), jnp.float32), jax.ShapeDtypeStruct(x.shape, x.dtype)) + held,
         in_specs=[VMEM_SPEC] * 2 + [HBM_SPEC] * 3,
-        out_specs=(VMEM_SPEC,) * 4,
+        out_specs=(VMEM_SPEC,) * 5,
         scratch_shapes=[pltpu.VMEM((rows, units), jnp.bfloat16), pltpu.SemaphoreType.DMA((3, len(unit_tiles(units))))],
         compiler_params=pltpu.CompilerParams(vmem_limit_bytes=OWN_VMEM_LIMIT),
         cost_estimate=cost(rows, width, units),
         name="own_block",
     )(x, scale, *weights)
-    return part, kept
+    return part, tokens, kept
 
 
 def arrived_block(x, scale, weights, dtype):
@@ -93,6 +123,21 @@
     )(x, scale, *weights)
 
 
+def arrived_and_own_block(x, scale, weights, dtype, held, own):
+    rows, width = x.shape
+    units = weights[0].shape[0]
+    return pl.pallas_call(
+        arrived_and_own_kernel,
+        out_shape=(jax.ShapeDtypeStruct((rows, width), dtype), jax.ShapeDtypeStruct((rows, width), jnp.float32)),
+        in_specs=[VMEM_SPEC] * 7,
+        out_specs=(VMEM_SPEC,) * 2,
+        scratch_shapes=[pltpu.VMEM((rows, units), jnp.bfloat16)],
+        compiler_params=pltpu.CompilerParams(vmem_limit_bytes=VMEM_LIMIT),
+        cost_estimate=cost(rows, width, units),
+        name="arrived_and_own_block",
+    )(x, scale, *weights, held, own)
+
+
 def hop(block, route, axes="tensor"):
     return lax.ppermute(block, axes, route)
 
@@ -101,7 +146,7 @@
     return (arrived.astype(jnp.float32) + part).astype(jnp.bfloat16)
 
 
-def line_of_four(tokens, own, scale, weights):
+def line_of_four(tokens, held, own, scale, weights):
     beside = [(place, place ^ 1) for place in range(4)]
     groups = range(lax.axis_size("dp"))
 
@@ -113,32 +158,34 @@
 
     x_1 = hop(tokens, beside)
     x_far, own = lax.optimization_barrier((far_hop(tokens, (2, 3)), own))
-    part_1 = arrived_block(x_1, scale, weights, jnp.bfloat16)
     x_last = hop(x_far, beside)
-    joining = hop(arrived_block(x_far, scale, weights, jnp.bfloat16), beside)
-    from_neighbour = hop(part_1, beside)
+    part_far, own = arrived_and_own_block(x_far, scale, weights, jnp.bfloat16, held, own)
+    joining = hop(part_far, beside)
+    from_neighbour = hop(arrived_block(x_1, scale, weights, jnp.bfloat16), beside)
     from_far = far_hop(add(joining, arrived_block(x_last, scale, weights, jnp.float32)), (3, 2))
     return (own + from_neighbour.astype(jnp.float32) + from_far.astype(jnp.float32)).astype(jnp.bfloat16)
 
 
-def folded_ring(tokens, own, scale, weights, n):
+def folded_ring(tokens, held, own, scale, weights, n):
     order = list(range(0, n, 2)) + list(range(1, n, 2))[::-1]
     route = [(order[k - 1], order[k]) for k in range(n)]
     x, summed = tokens, None
     for step in range(1, n):
         x = hop(x, route)
-        part = arrived_block(x, scale, weights, jnp.bfloat16 if step == 1 else jnp.float32)
-        summed = part if step == 1 else add(hop(summed, route), part)
-    return add(hop(summed, route), own) if n > 1 else own.astype(jnp.bfloat16)
+        if step == 1:
+            summed, own = arrived_and_own_block(x, scale, weights, jnp.bfloat16, held, own)
+        else:
+            summed = add(hop(summed, route), arrived_block(x, scale, weights, jnp.float32))
+    return add(hop(summed, route), own)
 
 
 def shards(tokens, smooth_scale, gate_weight, up_weight, down_weight):
     n = lax.axis_size("tensor")
     scale = smooth_scale[None, :]
-    own, weights = own_block(tokens, scale, (gate_weight, up_weight, down_weight))
+    own, held, weights = own_block(tokens, scale, (gate_weight, up_weight, down_weight))
     if n == 4:
-        return line_of_four(tokens, own, scale, weights)
-    return folded_ring(tokens, own, scale, weights, n)
+        return line_of_four(tokens, held, own, scale, weights)
+    return folded_ring(tokens, held, own, scale, weights, n)
 
 
 def solution(mesh):

time: 38 us -> 39.1 us (1.029)
  the two profiles are of different devices: /device:TPU:0 before, /device:TPU:1 now
where the time goes in v9:
time: 39.1 us; the launch traced here: 39 us
  waiting for transfers between devices  15.4 us (39%)
  Pallas kernels  10.8 us (28%)
  starting transfers between devices  10.2 us (26%)
  local copies, waits for them, and re-layouts  1.63 us (4%)
  other arithmetic  0.8 us (2%)
    ppermute x6, waiting for transfers between devices, hop(): return lax.ppermute(block, axes, route)  15.4 us
    ppermute x6, starting transfers between devices, hop(): return lax.ppermute(block, axes, route)  10.2 us
    pallas_call x1, Pallas kernels, arrived_and_own_block(): pl.pallas_call(arrived_and_own_kernel, out_shape=(jax.ShapeDtypeStruct((r...  3.89 us
    pallas_call x2, Pallas kernels, arrived_block(): pl.pallas_call(arrived_kernel, out_shape=jax.ShapeDtypeStruct((rows, widt...  3.82 us
    pallas_call x1, Pallas kernels, own_block(): pl.pallas_call(own_kernel, out_shape=(jax.ShapeDtypeStruct((rows, width),...  3.09 us
    unnamed x2, local copies, waits for them, and re-layouts  0.94 us
  transfers between devices with their start and end apart: 6, of which 4 were waited for; matrix products, arithmetic and copies ran while one was open for 2% of the time, Pallas kernels for 28%

profile of v9, /device:TPU:1, one launch (start us, length us, event | category | flops | bytes accessed | tf_op | source)
XLA Modules:
  0.0 39.0 jit_solution(2160662642615539809)
XLA Ops:
  0.0 4.2 %collective-permute-start = (bf16[128,896]{1,0:T(8,128)(2,1)}, bf16[128,896]{1,0:T(8,128)(2,1)S(1)}, u32[]{:S(2)}, u32[]{:S(2)}) collective-permute-start(bf16[128,896]{1,0:T(8,128)(2,1)} %x_ref.1), channel_id=1, source_target_pairs={{0,2},{1,3},{2,0},{3,1},{4,7},{5,6},{6,5},{7,4},{8,10},{9,11},{10,... | collective-permute-start | bytes 688136 | tf_op jit(solution)/shard_map/ppermute | solution.py:142
  4.2 0.0 collective-permute-start.1
  4.2 0.7 %broadcast_in_dim.3.scale_ref.refs_0_ = f32[1,896]{1,0:T(1,128)S(1)} reshape(f32[896]{0:T(1024)} %param.6) | data formatting | bytes 7168 | tf_op jit(solution)/shard_map/broadcast_in_dim | solution.py:184
  4.8 0.0 copy-start
  4.8 0.9 %copy-done = bf16[128,896]{1,0:T(8,128)(2,1)S(1)} copy-done((bf16[128,896]{1,0:T(8,128)(2,1)S(1)}, bf16[128,896]{1,0:T(8,128)(2,1)}, u32[]{:S(2)}) %copy-start) | copy-done | bytes 229400
  5.8 3.1 %own_block.1 = (f32[128,896]{1,0:T(8,128)S(1)}, bf16[128,896]{1,0:T(8,128)(2,1)S(1)}, bf16[1216,896]{1,0:T(8,128)(2,1)S(1)}, bf16[1216,896]{1,0:T(8,128)(2,1)S(1)}, bf16[1216,896]{1,0:T(8,128)(2,1)S(1)}) custom-call(bf16[128,896]{1,0:T(8,128)(2,1)S(1)} %copy-done, f32[1,896]{1,0:T(1,128)S(1)} %broadcast_in_dim.3.scale_ref.refs_0_, ...), custom_call_target="tpu_custom_call" | custom-call | flops 836763648 | bytes 6537216 | tf_op jit(solution)/shard_map/own_block/pallas_call | solution.py:98
  8.9 0.9 %collective-permute-done.x_ref = bf16[128,896]{1,0:T(8,128)(2,1)S(1)} collective-permute-done((bf16[128,896]{1,0:T(8,128)(2,1)}, bf16[128,896]{1,0:T(8,128)(2,1)S(1)}, u32[]{:S(2)}, u32[]{:S(2)}) %collective-permute-start) | collective-permute-done | bytes 229408 | tf_op jit(solution)/shard_map/ppermute | solution.py:142
  9.8 4.4 %collective-permute-start.4 = (bf16[128,896]{1,0:T(8,128)(2,1)S(1)}, bf16[128,896]{1,0:T(8,128)(2,1)S(1)}, u32[]{:S(2)}, u32[]{:S(2)}) collective-permute-start(bf16[128,896]{1,0:T(8,128)(2,1)S(1)} %collective-permute-done.x_ref), channel_id=1, source_target_pairs={{0,1},{1,0},{2,3},{3,2},{4,5},{5,4},{6,7},{7,6},{8,9},{9,8},{10,11... | collective-permute-start | bytes 688136 | tf_op jit(solution)/shard_map/ppermute | solution.py:142
  14.2 3.9 %arrived_and_own_block.1 = (bf16[128,896]{1,0:T(8,128)(2,1)S(1)}, f32[128,896]{1,0:T(8,128)S(1)}) custom-call(bf16[128,896]{1,0:T(8,128)(2,1)S(1)} %collective-permute-done.x_ref, f32[1,896]{1,0:T(1,128)S(1)} %broadcast_in_dim.3.scale_ref.refs_0_, bf16[1216,896]{1,0:T(8,128)(2,1)S(1)} %get-tuple-element.16.gate_ref.refs_1_, ...), custom_call_target="tpu_custom_call" | custom-call | flops 836763648 | bytes 6537216 | tf_op jit(solution)/shard_map/arrived_and_own_block/pallas_call | solution.py:129
  18.1 0.1 collective-permute-start.3
  18.2 0.0 collective-permute-done.1.x_ref
  18.2 1.9 %arrived_block.2 = bf16[128,896]{1,0:T(8,128)(2,1)S(1)} custom-call(bf16[128,896]{1,0:T(8,128)(2,1)S(1)} %collective-permute-done.1.x_ref, f32[1,896]{1,0:T(1,128)S(1)} %broadcast_in_dim.3.scale_ref.refs_0_, bf16[1216,896]{1,0:T(8,128)(2,1)S(1)} %get-tuple-element.16.gate_ref.refs_1_, bf16[1216,896]{1,0:T(8,128)(2,1)S(1)} %get-tuple-element.17.up_ref.refs_2_, ...), custom_call_target="tpu_custom_call" | custom-call | flops 836763648 | bytes 6537216 | tf_op jit(solution)/shard_map/arrived_block/pallas_call | solution.py:114
  20.1 1.5 %collective-permute-start.2 = (bf16[128,896]{1,0:T(8,128)(2,1)S(1)}, bf16[128,896]{1,0:T(8,128)(2,1)S(1)}, u32[]{:S(2)}, u32[]{:S(2)}) collective-permute-start(bf16[128,896]{1,0:T(8,128)(2,1)S(1)} %arrived_block.2), channel_id=1, source_target_pairs={{0,1},{1,0},{2,3},{3,2},{4,5},{5,4},{6,7},{7,6},{8,9},{9,8},{10,11... | collective-permute-start | bytes 688136 | tf_op jit(solution)/shard_map/ppermute | solution.py:142
  21.6 0.0 collective-permute-done.4.x_ref
  21.6 1.9 %arrived_block.3 = f32[128,896]{1,0:T(8,128)S(1)} custom-call(bf16[128,896]{1,0:T(8,128)(2,1)S(1)} %collective-permute-done.4.x_ref, f32[1,896]{1,0:T(1,128)S(1)} %broadcast_in_dim.3.scale_ref.refs_0_, bf16[1216,896]{1,0:T(8,128)(2,1)S(1)} %get-tuple-element.16.gate_ref.refs_1_, bf16[1216,896]{1,0:T(8,128)(2,1)S(1)} %get-tuple-element.17.up_ref.refs_2_, ...), custom_call_target="tpu_custom_call" | custom-call | flops 836763648 | bytes 6537216 | tf_op jit(solution)/shard_map/arrived_block/pallas_call | solution.py:114
  23.6 2.3 %collective-permute-done.3 = bf16[128,896]{1,0:T(8,128)(2,1)S(1)} collective-permute-done((bf16[128,896]{1,0:T(8,128)(2,1)S(1)}, bf16[128,896]{1,0:T(8,128)(2,1)S(1)}, u32[]{:S(2)}, u32[]{:S(2)}) %collective-permute-start.3) | collective-permute-done | bytes 229408 | tf_op jit(solution)/shard_map/ppermute | solution.py:142
  25.9 0.1 collective-permute-start.5
  26.0 5.1 %collective-permute-done.2 = bf16[128,896]{1,0:T(8,128)(2,1)S(1)} collective-permute-done((bf16[128,896]{1,0:T(8,128)(2,1)S(1)}, bf16[128,896]{1,0:T(8,128)(2,1)S(1)}, u32[]{:S(2)}, u32[]{:S(2)}) %collective-permute-start.2) | collective-permute-done | bytes 229408 | tf_op jit(solution)/shard_map/ppermute | solution.py:142
  31.1 7.1 %collective-permute-done.5 = bf16[128,896]{1,0:T(8,128)(2,1)S(1)} collective-permute-done((bf16[128,896]{1,0:T(8,128)(2,1)S(1)}, bf16[128,896]{1,0:T(8,128)(2,1)S(1)}, u32[]{:S(2)}, u32[]{:S(2)}) %collective-permute-start.5) | collective-permute-done | bytes 229408 | tf_op jit(solution)/shard_map/ppermute | solution.py:142
  38.2 0.8 %add_convert_fusion = bf16[128,896]{1,0:T(8,128)(2,1)} fusion(bf16[128,896]{1,0:T(8,128)(2,1)S(1)} %collective-permute-done.5, f32[128,896]{1,0:T(8,128)S(1)} %get-tuple-element.21, bf16[128,896]{1,0:T(8,128)(2,1)S(1)} %collective-permute-done.2), kind=kLoop, calls=%fused_computation | loop fusion | flops 573440 | bytes 1146880 | tf_op jit(solution)/shard_map/convert_element_type | solution.py:166
  (1 shorter events, 0.0 us)
Async XLA Ops:
  0.0 9.8 %collective-permute-start = (bf16[128,896]{1,0:T(8,128)(2,1)}, bf16[128,896]{1,0:T(8,128)(2,1)S(1)}, u32[]{:S(2)}, u32[]{:S(2)}) collective-permute-start(bf16[128,896]{1,0:T(8,128)(2,1)} %x_ref.1), channel_id=1, source_target_pairs={{0,2},{1,3},{2,0},{3,1},{4,7},{5,6},{6,5},{7,4},{8,10},{9,11},{10,... | collective-permute-start | bytes 688136 | tf_op jit(solution)/shard_map/ppermute | solution.py:142
  4.2 14.1 %collective-permute-start.1 = (bf16[128,896]{1,0:T(8,128)(2,1)}, bf16[128,896]{1,0:T(8,128)(2,1)S(1)}, u32[]{:S(2)}, u32[]{:S(2)}) collective-permute-start(bf16[128,896]{1,0:T(8,128)(2,1)} %x_ref.1), channel_id=1, source_target_pairs={{0,1},{1,0},{2,3},{3,2},{4,5},{5,4},{6,7},{7,6},{8,9},{9,8},{10,11... | collective-permute-start | bytes 688136 | tf_op jit(solution)/shard_map/ppermute | solution.py:142
  4.8 0.9 %copy-start = (bf16[128,896]{1,0:T(8,128)(2,1)S(1)}, bf16[128,896]{1,0:T(8,128)(2,1)}, u32[]{:S(2)}) copy-start(bf16[128,896]{1,0:T(8,128)(2,1)} %x_ref.1) | copy-start | bytes 688132
  9.8 11.8 %collective-permute-start.4 = (bf16[128,896]{1,0:T(8,128)(2,1)S(1)}, bf16[128,896]{1,0:T(8,128)(2,1)S(1)}, u32[]{:S(2)}, u32[]{:S(2)}) collective-permute-start(bf16[128,896]{1,0:T(8,128)(2,1)S(1)} %collective-permute-done.x_ref), channel_id=1, source_target_pairs={{0,1},{1,0},{2,3},{3,2},{4,5},{5,4},{6,7},{7,6},{8,9},{9,8},{10,11... | collective-permute-start | bytes 688136 | tf_op jit(solution)/shard_map/ppermute | solution.py:142
  18.1 7.8 %collective-permute-start.3 = (bf16[128,896]{1,0:T(8,128)(2,1)S(1)}, bf16[128,896]{1,0:T(8,128)(2,1)S(1)}, u32[]{:S(2)}, u32[]{:S(2)}) collective-permute-start(bf16[128,896]{1,0:T(8,128)(2,1)S(1)} %get-tuple-element.22), channel_id=1, source_target_pairs={{0,1},{1,0},{2,3},{3,2},{4,5},{5,4},{6,7},{7,6},{8,9},{9,8},{10,11... | collective-permute-start | bytes 688136 | tf_op jit(solution)/shard_map/ppermute | solution.py:142
  20.1 11.0 %collective-permute-start.2 = (bf16[128,896]{1,0:T(8,128)(2,1)S(1)}, bf16[128,896]{1,0:T(8,128)(2,1)S(1)}, u32[]{:S(2)}, u32[]{:S(2)}) collective-permute-start(bf16[128,896]{1,0:T(8,128)(2,1)S(1)} %arrived_block.2), channel_id=1, source_target_pairs={{0,1},{1,0},{2,3},{3,2},{4,5},{5,4},{6,7},{7,6},{8,9},{9,8},{10,11... | collective-permute-start | bytes 688136 | tf_op jit(solution)/shard_map/ppermute | solution.py:142
  25.9 12.3 %collective-permute-start.5 = (bf16[128,896]{1,0:T(8,128)(2,1)S(1)}, bf16[128,896]{1,0:T(8,128)(2,1)S(1)}, u32[]{:S(2)}, u32[]{:S(2)}) collective-permute-start(bf16[128,896]{1,0:T(8,128)(2,1)S(1)} %add_convert_fusion.1), channel_id=1, source_target_pairs={{0,3},{1,2},{2,1},{3,0},{4,6},{5,7},{6,4},{7,5},{8,11},{9,10},{10,... | collective-permute-start | bytes 688136 | tf_op jit(solution)/shard_map/ppermute | solution.py:142

commit v10 on v7

--- a/solution.py
+++ b/solution.py
@@ -115,10 +115,12 @@
     x_far, own = lax.optimization_barrier((far_hop(tokens, (2, 3)), own))
     part_1 = arrived_block(x_1, scale, weights, jnp.bfloat16)
     x_last = hop(x_far, beside)
-    joining = hop(arrived_block(x_far, scale, weights, jnp.bfloat16), beside)
+    from_first = far_hop(arrived_block(x_far, scale, weights, jnp.bfloat16), (2, 3))
     from_neighbour = hop(part_1, beside)
-    from_far = far_hop(add(joining, arrived_block(x_last, scale, weights, jnp.float32)), (3, 2))
-    return (own + from_neighbour.astype(jnp.float32) + from_far.astype(jnp.float32)).astype(jnp.bfloat16)
+    from_last = far_hop(arrived_block(x_last, scale, weights, jnp.bfloat16), (3, 2))
+    for arrived in (from_first, from_neighbour, from_last):
+        own = own + arrived.astype(jnp.float32)
+    return own.astype(jnp.bfloat16)
 
 
 def folded_ring(tokens, own, scale, weights, n):

time: 38 us -> 37.3 us (0.982)
  starting transfers between devices: 12.7 us -> 10.5 us
  waiting for transfers between devices: 12.6 us -> 14.4 us
    ppermute x6, starting transfers between devices: 12.7 us -> 10.5 us  [hop(): return lax.ppermute(block, axes, route)]
    ppermute x6, waiting for transfers between devices: 12.6 us -> 14.4 us  [hop(): return lax.ppermute(block, axes, route)]
    convert_element_type x2 -> x1, other arithmetic: 0.8 us -> 0.79 us  [line_of_four(): return own.astype(jnp.bfloat16)]
  transfers between devices with their start and end apart: 6 -> 6, of which waited for: 5 -> 4; matrix products, arithmetic and copies ran while one was open for 2% -> 2% of each run, Pallas kernels for 26% -> 26%
where the time goes in v10:
time: 37.3 us; the launch traced here: 37.2 us
  waiting for transfers between devices  14.4 us (39%)
  starting transfers between devices  10.5 us (28%)
  Pallas kernels  9.78 us (26%)
  local copies, waits for them, and re-layouts  1.63 us (4%)
  other arithmetic  0.79 us (2%)
    ppermute x6, waiting for transfers between devices, hop(): return lax.ppermute(block, axes, route)  14.4 us
    ppermute x6, starting transfers between devices, hop(): return lax.ppermute(block, axes, route)  10.5 us
    pallas_call x3, Pallas kernels, arrived_block(): pl.pallas_call(arrived_kernel, out_shape=jax.ShapeDtypeStruct((rows, widt...  5.73 us
    pallas_call x1, Pallas kernels, own_block(): pl.pallas_call(own_kernel, out_shape=(jax.ShapeDtypeStruct((rows, width),...  4.04 us
    unnamed x2, local copies, waits for them, and re-layouts  0.94 us
    convert_element_type x1, other arithmetic, line_of_four(): return own.astype(jnp.bfloat16)  0.79 us
  transfers between devices with their start and end apart: 6, of which 4 were waited for; matrix products, arithmetic and copies ran while one was open for 2% of the time, Pallas kernels for 26%

profile of v10, /device:TPU:0, one launch (start us, length us, event | category | flops | bytes accessed | tf_op | source)
XLA Modules:
  0.0 37.2 jit_solution(13117713297386151752)
XLA Ops:
  0.0 4.0 %collective-permute-start = (bf16[128,896]{1,0:T(8,128)(2,1)}, bf16[128,896]{1,0:T(8,128)(2,1)S(1)}, u32[]{:S(2)}, u32[]{:S(2)}) collective-permute-start(bf16[128,896]{1,0:T(8,128)(2,1)} %x_ref.1), channel_id=1, source_target_pairs={{0,2},{1,3},{2,0},{3,1},{4,7},{5,6},{6,5},{7,4},{8,10},{9,11},{10,... | collective-permute-start | bytes 688136 | tf_op jit(solution)/shard_map/ppermute | solution.py:97
  4.0 1.6 %collective-permute-start.2 = (bf16[128,896]{1,0:T(8,128)(2,1)}, bf16[128,896]{1,0:T(8,128)(2,1)S(1)}, u32[]{:S(2)}, u32[]{:S(2)}) collective-permute-start(bf16[128,896]{1,0:T(8,128)(2,1)} %x_ref.1), channel_id=1, source_target_pairs={{0,1},{1,0},{2,3},{3,2},{4,5},{5,4},{6,7},{7,6},{8,9},{9,8},{10,11... | collective-permute-start | bytes 688136 | tf_op jit(solution)/shard_map/ppermute | solution.py:97
  5.6 0.7 %broadcast_in_dim.3.scale_ref = f32[1,896]{1,0:T(1,128)S(1)} reshape(f32[896]{0:T(1024)} %param.6) | data formatting | bytes 7168 | tf_op jit(solution)/shard_map/broadcast_in_dim | solution.py:139
  6.3 0.0 copy-start
  6.3 0.9 %copy-done = bf16[128,896]{1,0:T(8,128)(2,1)S(1)} copy-done((bf16[128,896]{1,0:T(8,128)(2,1)S(1)}, bf16[128,896]{1,0:T(8,128)(2,1)}, u32[]{:S(2)}) %copy-start) | copy-done | bytes 229400
  7.2 4.0 %own_block.1 = (f32[128,896]{1,0:T(8,128)S(1)}, bf16[1216,896]{1,0:T(8,128)(2,1)S(1)}, bf16[1216,896]{1,0:T(8,128)(2,1)S(1)}, bf16[1216,896]{1,0:T(8,128)(2,1)S(1)}) custom-call(bf16[128,896]{1,0:T(8,128)(2,1)S(1)} %copy-done, f32[1,896]{1,0:T(1,128)S(1)} %broadcast_in_dim.3.scale_ref, bf16[1216,896]{1,0:T(8,128)(2,1)} %gate_hbm.1, ...), custom_call_target="tpu_custom_call" | custom-call | flops 836763648 | bytes 6537216 | tf_op jit(solution)/shard_map/own_block/pallas_call | solution.py:68
  11.3 3.7 %collective-permute-done.x_ref = bf16[128,896]{1,0:T(8,128)(2,1)S(1)} collective-permute-done((bf16[128,896]{1,0:T(8,128)(2,1)}, bf16[128,896]{1,0:T(8,128)(2,1)S(1)}, u32[]{:S(2)}, u32[]{:S(2)}) %collective-permute-start) | collective-permute-done | bytes 229408 | tf_op jit(solution)/shard_map/ppermute | solution.py:97
  15.0 0.0 collective-permute-start.4
  15.0 1.9 %arrived_block.3 = bf16[128,896]{1,0:T(8,128)(2,1)S(1)} custom-call(bf16[128,896]{1,0:T(8,128)(2,1)S(1)} %collective-permute-done.x_ref, f32[1,896]{1,0:T(1,128)S(1)} %broadcast_in_dim.3.scale_ref, bf16[1216,896]{1,0:T(8,128)(2,1)S(1)} %get-tuple-element.14.gate_ref, bf16[1216,896]{1,0:T(8,128)(2,1)S(1)} %get-tuple-element.15.up_ref, ...), custom_call_target="tpu_custom_call" | custom-call | flops 836763648 | bytes 6537216 | tf_op jit(solution)/shard_map/arrived_block/pallas_call | solution.py:84
  17.0 3.1 %collective-permute-start.1 = (bf16[128,896]{1,0:T(8,128)(2,1)S(1)}, bf16[128,896]{1,0:T(8,128)(2,1)S(1)}, u32[]{:S(2)}, u32[]{:S(2)}) collective-permute-start(bf16[128,896]{1,0:T(8,128)(2,1)S(1)} %arrived_block.3), channel_id=1, source_target_pairs={{0,2},{1,3},{2,0},{3,1},{4,7},{5,6},{6,5},{7,4},{8,10},{9,11},{10,... | collective-permute-start | bytes 688136 | tf_op jit(solution)/shard_map/ppermute | solution.py:97
  20.0 0.0 collective-permute-done.2.x_ref
  20.0 1.9 %arrived_block.4 = bf16[128,896]{1,0:T(8,128)(2,1)S(1)} custom-call(bf16[128,896]{1,0:T(8,128)(2,1)S(1)} %collective-permute-done.2.x_ref, f32[1,896]{1,0:T(1,128)S(1)} %broadcast_in_dim.3.scale_ref, bf16[1216,896]{1,0:T(8,128)(2,1)S(1)} %get-tuple-element.14.gate_ref, bf16[1216,896]{1,0:T(8,128)(2,1)S(1)} %get-tuple-element.15.up_ref, ...), custom_call_target="tpu_custom_call" | custom-call | flops 836763648 | bytes 6537216 | tf_op jit(solution)/shard_map/arrived_block/pallas_call | solution.py:84
  21.9 0.1 collective-permute-start.3
  22.0 0.0 collective-permute-done.4.x_ref
  22.0 1.9 %arrived_block.5 = bf16[128,896]{1,0:T(8,128)(2,1)S(1)} custom-call(bf16[128,896]{1,0:T(8,128)(2,1)S(1)} %collective-permute-done.4.x_ref, f32[1,896]{1,0:T(1,128)S(1)} %broadcast_in_dim.3.scale_ref, bf16[1216,896]{1,0:T(8,128)(2,1)S(1)} %get-tuple-element.14.gate_ref, bf16[1216,896]{1,0:T(8,128)(2,1)S(1)} %get-tuple-element.15.up_ref, ...), custom_call_target="tpu_custom_call" | custom-call | flops 836763648 | bytes 6537216 | tf_op jit(solution)/shard_map/arrived_block/pallas_call | solution.py:84
  23.9 1.8 %collective-permute-start.5 = (bf16[128,896]{1,0:T(8,128)(2,1)S(1)}, bf16[128,896]{1,0:T(8,128)(2,1)S(1)}, u32[]{:S(2)}, u32[]{:S(2)}) collective-permute-start(bf16[128,896]{1,0:T(8,128)(2,1)S(1)} %arrived_block.5), channel_id=1, source_target_pairs={{0,3},{1,2},{2,1},{3,0},{4,6},{5,7},{6,4},{7,5},{8,11},{9,10},{10,... | collective-permute-start | bytes 688136 | tf_op jit(solution)/shard_map/ppermute | solution.py:97
  25.7 6.4 %collective-permute-done.1 = bf16[128,896]{1,0:T(8,128)(2,1)S(1)} collective-permute-done((bf16[128,896]{1,0:T(8,128)(2,1)S(1)}, bf16[128,896]{1,0:T(8,128)(2,1)S(1)}, u32[]{:S(2)}, u32[]{:S(2)}) %collective-permute-start.1) | collective-permute-done | bytes 229408 | tf_op jit(solution)/shard_map/ppermute | solution.py:97
  32.1 2.3 %collective-permute-done.3 = bf16[128,896]{1,0:T(8,128)(2,1)S(1)} collective-permute-done((bf16[128,896]{1,0:T(8,128)(2,1)S(1)}, bf16[128,896]{1,0:T(8,128)(2,1)S(1)}, u32[]{:S(2)}, u32[]{:S(2)}) %collective-permute-start.3) | collective-permute-done | bytes 229408 | tf_op jit(solution)/shard_map/ppermute | solution.py:97
  34.4 2.0 %collective-permute-done.5 = bf16[128,896]{1,0:T(8,128)(2,1)S(1)} collective-permute-done((bf16[128,896]{1,0:T(8,128)(2,1)S(1)}, bf16[128,896]{1,0:T(8,128)(2,1)S(1)}, u32[]{:S(2)}, u32[]{:S(2)}) %collective-permute-start.5) | collective-permute-done | bytes 229408 | tf_op jit(solution)/shard_map/ppermute | solution.py:97
  36.4 0.8 %add_convert_fusion = bf16[128,896]{1,0:T(8,128)(2,1)} fusion(bf16[128,896]{1,0:T(8,128)(2,1)S(1)} %collective-permute-done.5, bf16[128,896]{1,0:T(8,128)(2,1)S(1)} %collective-permute-done.3, f32[128,896]{1,0:T(8,128)S(1)} %get-tuple-element.12, bf16[128,896]{1,0:T(8,128)(2,1)S(1)} %collective-permute-done.1), kind=kLoop, calls=%fused_computation | loop fusion | flops 802816 | bytes 1376256 | tf_op jit(solution)/shard_map/convert_element_type | solution.py:123
Async XLA Ops:
  0.0 15.0 %collective-permute-start = (bf16[128,896]{1,0:T(8,128)(2,1)}, bf16[128,896]{1,0:T(8,128)(2,1)S(1)}, u32[]{:S(2)}, u32[]{:S(2)}) collective-permute-start(bf16[128,896]{1,0:T(8,128)(2,1)} %x_ref.1), channel_id=1, source_target_pairs={{0,2},{1,3},{2,0},{3,1},{4,7},{5,6},{6,5},{7,4},{8,10},{9,11},{10,... | collective-permute-start | bytes 688136 | tf_op jit(solution)/shard_map/ppermute | solution.py:97
  4.0 16.0 %collective-permute-start.2 = (bf16[128,896]{1,0:T(8,128)(2,1)}, bf16[128,896]{1,0:T(8,128)(2,1)S(1)}, u32[]{:S(2)}, u32[]{:S(2)}) collective-permute-start(bf16[128,896]{1,0:T(8,128)(2,1)} %x_ref.1), channel_id=1, source_target_pairs={{0,1},{1,0},{2,3},{3,2},{4,5},{5,4},{6,7},{7,6},{8,9},{9,8},{10,11... | collective-permute-start | bytes 688136 | tf_op jit(solution)/shard_map/ppermute | solution.py:97
  6.3 0.9 %copy-start = (bf16[128,896]{1,0:T(8,128)(2,1)S(1)}, bf16[128,896]{1,0:T(8,128)(2,1)}, u32[]{:S(2)}) copy-start(bf16[128,896]{1,0:T(8,128)(2,1)} %x_ref.1) | copy-start | bytes 688132
  15.0 7.0 %collective-permute-start.4 = (bf16[128,896]{1,0:T(8,128)(2,1)S(1)}, bf16[128,896]{1,0:T(8,128)(2,1)S(1)}, u32[]{:S(2)}, u32[]{:S(2)}) collective-permute-start(bf16[128,896]{1,0:T(8,128)(2,1)S(1)} %collective-permute-done.x_ref), channel_id=1, source_target_pairs={{0,1},{1,0},{2,3},{3,2},{4,5},{5,4},{6,7},{7,6},{8,9},{9,8},{10,11... | collective-permute-start | bytes 688136 | tf_op jit(solution)/shard_map/ppermute | solution.py:97
  17.0 15.1 %collective-permute-start.1 = (bf16[128,896]{1,0:T(8,128)(2,1)S(1)}, bf16[128,896]{1,0:T(8,128)(2,1)S(1)}, u32[]{:S(2)}, u32[]{:S(2)}) collective-permute-start(bf16[128,896]{1,0:T(8,128)(2,1)S(1)} %arrived_block.3), channel_id=1, source_target_pairs={{0,2},{1,3},{2,0},{3,1},{4,7},{5,6},{6,5},{7,4},{8,10},{9,11},{10,... | collective-permute-start | bytes 688136 | tf_op jit(solution)/shard_map/ppermute | solution.py:97
  21.9 12.5 %collective-permute-start.3 = (bf16[128,896]{1,0:T(8,128)(2,1)S(1)}, bf16[128,896]{1,0:T(8,128)(2,1)S(1)}, u32[]{:S(2)}, u32[]{:S(2)}) collective-permute-start(bf16[128,896]{1,0:T(8,128)(2,1)S(1)} %arrived_block.4), channel_id=1, source_target_pairs={{0,1},{1,0},{2,3},{3,2},{4,5},{5,4},{6,7},{7,6},{8,9},{9,8},{10,11... | collective-permute-start | bytes 688136 | tf_op jit(solution)/shard_map/ppermute | solution.py:97
  23.9 12.4 %collective-permute-start.5 = (bf16[128,896]{1,0:T(8,128)(2,1)S(1)}, bf16[128,896]{1,0:T(8,128)(2,1)S(1)}, u32[]{:S(2)}, u32[]{:S(2)}) collective-permute-start(bf16[128,896]{1,0:T(8,128)(2,1)S(1)} %arrived_block.5), channel_id=1, source_target_pairs={{0,3},{1,2},{2,1},{3,0},{4,6},{5,7},{6,4},{7,5},{8,11},{9,10},{10,... | collective-permute-start | bytes 688136 | tf_op jit(solution)/shard_map/ppermute | solution.py:97
